TPU v7x, 512 devices: a whole 4x4x16 slice. The times are simulated.
512 devices in a mesh: dom: 128 (over y, z, core), cell: 4 (over x).
Axes of the slice: x: 4, y: 4, z: 16, core: 2. Of those that a mesh axis runs over, the one named last changes fastest.
Arguments:
- potential: float32 [64, 131072], P(None, ('dom', 'cell')), may hold values from -6 to 6
- types: int32 [131072, 1], P(('dom', 'cell')), may hold values from 0 to 127; in each aligned block of 256 rows (0 to 255, 256 to 511, ...) at most 4 rows name the same one
- saturation: int32 [131072], P(('dom', 'cell')), may hold values from 0 to 3
- pattern: int32 [131072], P(('dom', 'cell')), may hold values from 0 to 127
- inverses: bfloat16 [128, 4, 64, 64], P('dom'), may hold values from -1 to 1, as said below
- coupling: bfloat16 [128, 64, 64], P('dom'), may hold values from -0.75 to 0.75
- skin: float32 [8], replicated, may hold values from 0.25 to 1.75
Outputs:
- new_potential: float32 [64, 131072], P(None, ('dom', 'cell'))
Inputs may be any that keep to these rules, and one draw needn't show every extreme that they name: `types`: among the 256 points of one device no type is named more than 4 times. `inverses`: entries of the inverse blocks are bounded by 1.
All inputs are finite; a program needn't handle non-finite values.
Results may differ from a plain program's by a relative error of at most 0.0051.
Values may be sent and summed in bfloat16 or wider, within the bound.
A program may use at most 64 MiB of HBM per device.

v0:
```python
import jax
import jax.numpy as jnp
from jax import lax
from jax.sharding import PartitionSpec as P

ITERS = 3


def padded_2(array, sides, width):
    for axis, dim in sides:
        devices, length = (lax.axis_size(axis), array.shape[dim])
        up = [(i, (i + 1) % devices) for i in range(devices - 1)]
        down = [(j, i) for i, j in up]
        last = lax.slice_in_dim(array, length - width, length, axis=dim)
        leading = lax.slice_in_dim(array, 0, width, axis=dim)
        before = lax.ppermute(last, axis, up)
        after = lax.ppermute(leading, axis, down)
        array = jnp.concatenate([before, array, after], axis=dim)
    return array


def solve_slots(received, codes, inverses, coupling, skin):
    width = received.shape[0]
    count = received.shape[1] * received.shape[2]
    lam = skin.shape[0]
    levels = inverses.shape[1]
    drive = received.reshape(width, count)
    code_ints = codes.reshape(2, count).astype(jnp.int32)
    sat_level = code_ints[0]
    pat_bits = code_ints[1]
    shifts = jnp.arange(lam, dtype=jnp.int32)
    lam_index = shifts[:, None]
    raw_bits = jnp.bitwise_and(jnp.right_shift(pat_bits[None, :], lam_index), 1).astype(jnp.float32)
    bits_upward = jnp.where(lam_index < lam - 1, raw_bits, 0.0).reshape(1, lam * count)
    below_bits = jnp.bitwise_and(
        jnp.right_shift(pat_bits[None, :], jnp.maximum(lam_index - 1, 0)), 1
    ).astype(jnp.float32)
    bits_downward = jnp.where(lam_index > 0, below_bits, 0.0).reshape(1, lam * count)
    pick = (sat_level[None, :] == jnp.arange(levels, dtype=jnp.int32)[:, None]).astype(jnp.float32)
    pick_flat = jnp.tile(pick, (1, lam))
    couple = coupling[0]
    bvec = (skin[:, None] * jnp.ones((lam, count), jnp.float32)).reshape(1, lam * count) * jnp.tile(
        drive.astype(jnp.float32), (1, lam)
    )
    state = jnp.zeros((width, lam * count), jnp.float32)
    for sweep in range(ITERS):
        flat = state.astype(jnp.bfloat16)
        upper = jnp.dot(couple, flat, preferred_element_type=jnp.float32)
        lower = lax.dot_general(
            couple, flat, (((0,), (0,)), ((), ())), preferred_element_type=jnp.float32
        )
        upper_next = jnp.pad(upper[:, count:], ((0, 0), (0, count)))
        lower_prev = jnp.pad(lower[:, :-count], ((0, 0), (count, 0)))
        resid = bvec - bits_upward * upper_next - bits_downward * lower_prev
        rflat = resid.astype(jnp.bfloat16)
        state = jnp.zeros((width, lam * count), jnp.float32)
        for level in range(levels):
            term = jnp.dot(inverses[0, level], rflat, preferred_element_type=jnp.float32)
            state = state + term * pick_flat[level][None, :]
    return (jnp.sum(state.reshape(width, lam, count), axis=1) / lam).astype(jnp.bfloat16)


def body(potential, types, saturation, pattern, inverses, coupling, skin):
    width, points = potential.shape
    owners = lax.axis_size("dom")
    slots = max(2, 2 * points // owners)
    padded = padded_2(potential, ((("dom", "cell"), 1),), 1)
    dest = types[:, 0]
    onehot = (dest[:, None] == jnp.arange(owners, dtype=jnp.int32)[None, :]).astype(jnp.int32)
    ranks = jnp.sum((jnp.cumsum(onehot, axis=0) - 1) * onehot, axis=1)
    target = dest * slots + ranks
    placing = (target[:, None] == jnp.arange(owners * slots, dtype=jnp.int32)[None, :]).astype(
        jnp.bfloat16
    )
    drive = potential.astype(jnp.bfloat16)
    codes = jnp.stack([saturation, pattern]).astype(jnp.bfloat16)
    send_drive = (
        jnp.dot(drive, placing, preferred_element_type=jnp.float32)
        .astype(jnp.bfloat16)
        .reshape(width, owners, slots)
    )
    send_codes = (
        jnp.dot(codes, placing, preferred_element_type=jnp.float32)
        .astype(jnp.bfloat16)
        .reshape(2, owners, slots)
    )
    received = lax.all_to_all(send_drive, "dom", split_axis=1, concat_axis=1, tiled=True)
    recv_codes = lax.all_to_all(send_codes, "dom", split_axis=1, concat_axis=1, tiled=True)
    answer = solve_slots(received, recv_codes, inverses, coupling, skin)
    answer = answer.reshape(received.shape)
    back = lax.all_to_all(answer, "dom", split_axis=1, concat_axis=1, tiled=True)
    response = lax.dot_general(
        back.reshape(width, owners * slots),
        placing,
        (((1,), (1,)), ((), ())),
        preferred_element_type=jnp.float32,
    )
    stencil = padded[:, :-2] - 2.0 * potential + padded[:, 2:]
    return potential + 0.25 * stencil - response


def solution(mesh):
    placed = (
        P(None, ("dom", "cell")),
        P(("dom", "cell"), None),
        P(("dom", "cell")),
        P(("dom", "cell")),
        P("dom", None, None, None),
        P("dom", None, None),
        P(),
    )
    return jax.shard_map(
        body, mesh=mesh, in_specs=placed, out_specs=P(None, ("dom", "cell")), check_vma=False
    )
```

profile of v0, /device:TPU:1, one launch (start us, length us, event | category | flops | bytes accessed | tf_op | source)
XLA Modules:
  0.0 93.7 jit_solution(7291646791054281934)
XLA Ops:
  0.0 0.7 copy-done.5
  1.4 0.7 copy-done.7
  2.0 0.7 copy-done.8
  3.1 0.7 copy.17
  3.8 20.6 %all-to-all-start.1 = ((bf16[2,128,4]{2,0,1:T(2,128)(2,1)}), bf16[2,128,4]{2,0,1:T(2,128)(2,1)S(1)}, u32[]{:S(2)}, u32[]{:S(2)}) async-start(bf16[2,128,4]{2,0,1:T(2,128)(2,1)} %copy.17), calls=%async_computation.1 | async-start | bytes 131072 | tf_op jit(solution)/shard_map/all_to_all | solution.py:88
  25.0 0.6 copy-done.4
  25.6 0.3 fusion.11
  25.9 0.4 copy-done.6
  26.4 0.8 reshape.215
  27.2 12.2 %all-to-all-done.1 = bf16[2,128,4]{2,0,1:T(2,128)(2,1)S(1)} async-done(((bf16[2,128,4]{2,0,1:T(2,128)(2,1)}), bf16[2,128,4]{2,0,1:T(2,128)(2,1)S(1)}, u32[]{:S(2)}, u32[]{:S(2)}) %all-to-all-start.1) | async-done | bytes 2080 | tf_op jit(solution)/shard_map/all_to_all | solution.py:88
  39.4 6.5 %all-to-all-start = ((bf16[128,2,128]{2,1,0:T(2,128)(2,1)}), bf16[128,2,128]{2,1,0:T(2,128)(2,1)S(1)}, u32[]{:S(2)}, u32[]{:S(2)}) async-start(bf16[128,2,128]{2,1,0:T(2,128)(2,1)} %reshape.215), calls=%async_computation | async-start | bytes 131072 | tf_op jit(solution)/shard_map/all_to_all | solution.py:87
  46.0 0.4 slice_reduce_fusion
  46.8 14.2 %all-to-all-done = bf16[128,2,128]{2,1,0:T(2,128)(2,1)S(1)} async-done(((bf16[128,2,128]{2,1,0:T(2,128)(2,1)}), bf16[128,2,128]{2,1,0:T(2,128)(2,1)S(1)}, u32[]{:S(2)}, u32[]{:S(2)}) %all-to-all-start) | async-done | bytes 65568 | tf_op jit(solution)/shard_map/all_to_all | solution.py:87
  61.4 0.6 copy.20
  62.0 0.6 slice-done
  63.1 0.6 copy-done.3
  63.7 0.3 convolution_multiply_fusion.10
  64.2 0.3 convolution_multiply_fusion.8
  64.5 0.4 fusion.10
  65.2 0.3 convolution_bitcast_fusion.4
  65.9 0.3 convolution_multiply_fusion.6
  66.5 0.3 convolution_multiply_fusion.4
  66.7 0.4 fusion.9
  67.4 0.3 convolution_bitcast_fusion.3
  69.0 0.3 fusion.8
  69.3 0.6 copy.27
  70.3 0.8 reshape.217
  71.0 6.5 %all-to-all-start.2 = ((bf16[128,2,128]{2,1,0:T(2,128)(2,1)}), bf16[128,2,128]{2,1,0:T(2,128)(2,1)S(1)}, u32[]{:S(2)}, u32[]{:S(2)}) async-start(bf16[128,2,128]{2,1,0:T(2,128)(2,1)} %reshape.217), calls=%async_computation.2 | async-start | bytes 131072 | tf_op jit(solution)/shard_map/all_to_all | solution.py:91
  77.7 3.1 %collective-permute-start = (f32[64,1]{1,0:T(8,128)S(1)}, f32[64,1]{1,0:T(8,128)S(1)}, u32[]{:S(2)}, u32[]{:S(2)}) collective-permute-start(f32[64,1]{1,0:T(8,128)S(1)} %get-tuple-element.7), channel_id=1, source_target_pairs={{0,1},{1,2},{2,3},{3,4},{4,5},{5,6},{6,7},{7,8},{8,9},{9,10},{10,1... | collective-permute-start | bytes 776 | tf_op jit(solution)/shard_map/ppermute | solution.py:16
  80.8 4.1 %collective-permute-start.1 = (f32[64,1]{1,0:T(8,128)S(1)}, f32[64,1]{1,0:T(8,128)S(1)}, u32[]{:S(2)}, u32[]{:S(2)}) collective-permute-start(f32[64,1]{1,0:T(8,128)S(1)} %get-tuple-element.8), channel_id=1, source_target_pairs={{1,0},{2,1},{3,2},{4,3},{5,4},{6,5},{7,6},{8,7},{9,8},{10,9},{11,1... | collective-permute-start | bytes 776 | tf_op jit(solution)/shard_map/ppermute | solution.py:17
  84.9 7.8 %all-to-all-done.2 = bf16[128,2,128]{2,1,0:T(2,128)(2,1)S(1)} async-done(((bf16[128,2,128]{2,1,0:T(2,128)(2,1)}), bf16[128,2,128]{2,1,0:T(2,128)(2,1)S(1)}, u32[]{:S(2)}, u32[]{:S(2)}) %all-to-all-start.2) | async-done | bytes 65568 | tf_op jit(solution)/shard_map/all_to_all | solution.py:91
  92.8 0.9 fusion.24
  (77 shorter events, 6.2 us)
Async XLA Ops:
  0.0 24.4 %copy-start = (bf16[1,64,64]{2,1,0:T(8,128)(2,1)S(1)}, bf16[1,64,64]{2,1,0:T(8,128)(2,1)}, u32[]{:S(2)}) copy-start(bf16[1,64,64]{2,1,0:T(8,128)(2,1)} %param.12) | copy-start | bytes 24580
  0.0 0.7 copy-start.5
  1.3 0.7 copy-start.7
  2.0 0.7 copy-start.8
  3.8 35.6 %all-to-all-start.1 = ((bf16[2,128,4]{2,0,1:T(2,128)(2,1)}), bf16[2,128,4]{2,0,1:T(2,128)(2,1)S(1)}, u32[]{:S(2)}, u32[]{:S(2)}) async-start(bf16[2,128,4]{2,0,1:T(2,128)(2,1)} %copy.17), calls=%async_computation.1 | async-start | bytes 131072 | tf_op jit(solution)/shard_map/all_to_all | solution.py:88
  24.7 2.5 %copy-start.2 = (f32[64,4096]{1,0:T(8,128)}, f32[64,4096]{1,0:T(8,128)S(1)}, u32[]{:S(2)}) copy-start(f32[64,4096]{1,0:T(8,128)S(1)} %convolution_bitcast_fusion.2) | copy-start | bytes 3145732
  24.7 0.9 copy-start.4
  25.6 1.6 %copy-start.1 = (f32[64,4096]{1,0:T(8,128)}, f32[64,4096]{1,0:T(8,128)S(1)}, u32[]{:S(2)}) copy-start(f32[64,4096]{1,0:T(8,128)S(1)} %convolution_bitcast_fusion.5) | copy-start | bytes 3145732
  25.6 0.7 copy-start.6
  39.4 21.6 %all-to-all-start = ((bf16[128,2,128]{2,1,0:T(2,128)(2,1)}), bf16[128,2,128]{2,1,0:T(2,128)(2,1)S(1)}, u32[]{:S(2)}, u32[]{:S(2)}) async-start(bf16[128,2,128]{2,1,0:T(2,128)(2,1)} %reshape.215), calls=%async_computation | async-start | bytes 131072 | tf_op jit(solution)/shard_map/all_to_all | solution.py:87
  61.4 1.2 %slice-start = ((f32[64,4096]{1,0:T(8,128)}), f32[64,3584]{1,0:T(8,128)S(1)}, s32[]{:S(2)}) async-start(f32[64,4096]{1,0:T(8,128)} %copy-done.1), calls=%async_computation.3 | async-start | bytes 1835008 | tf_op jit(solution)/shard_map/slice | solution.py:53
  61.4 1.5 %slice-start.1 = ((f32[64,4096]{1,0:T(8,128)}), f32[64,3584]{1,0:T(8,128)S(1)}, s32[]{:S(2)}) async-start(f32[64,4096]{1,0:T(8,128)} %copy-done.2), calls=%async_computation.4 | async-start | bytes 1835008 | tf_op jit(solution)/shard_map/slice | solution.py:52
  62.8 0.8 copy-start.3
  71.0 21.6 %all-to-all-start.2 = ((bf16[128,2,128]{2,1,0:T(2,128)(2,1)}), bf16[128,2,128]{2,1,0:T(2,128)(2,1)S(1)}, u32[]{:S(2)}, u32[]{:S(2)}) async-start(bf16[128,2,128]{2,1,0:T(2,128)(2,1)} %reshape.217), calls=%async_computation.2 | async-start | bytes 131072 | tf_op jit(solution)/shard_map/all_to_all | solution.py:91
  77.7 15.1 %collective-permute-start = (f32[64,1]{1,0:T(8,128)S(1)}, f32[64,1]{1,0:T(8,128)S(1)}, u32[]{:S(2)}, u32[]{:S(2)}) collective-permute-start(f32[64,1]{1,0:T(8,128)S(1)} %get-tuple-element.7), channel_id=1, source_target_pairs={{0,1},{1,2},{2,3},{3,4},{4,5},{5,6},{6,7},{7,8},{8,9},{9,10},{10,1... | collective-permute-start | bytes 776 | tf_op jit(solution)/shard_map/ppermute | solution.py:16
  80.8 12.0 %collective-permute-start.1 = (f32[64,1]{1,0:T(8,128)S(1)}, f32[64,1]{1,0:T(8,128)S(1)}, u32[]{:S(2)}, u32[]{:S(2)}) collective-permute-start(f32[64,1]{1,0:T(8,128)S(1)} %get-tuple-element.8), channel_id=1, source_target_pairs={{1,0},{2,1},{3,2},{4,3},{5,4},{6,5},{7,6},{8,7},{9,8},{10,9},{11,1... | collective-permute-start | bytes 776 | tf_op jit(solution)/shard_map/ppermute | solution.py:17
where the time goes:
time: 94.2 us; the launch traced here: 93.7 us
  starting transfers between devices  40.8 us (43%)
  waiting for transfers between devices  34.2 us (36%)
  local copies, waits for them, and re-layouts  9.88 us (10%)
  matrix products  6.7 us (7%)
  other arithmetic  1.58 us (2%)
    all_to_all x1, starting transfers between devices, body(): lax.all_to_all(send_codes, 'dom', split_axis=1, concat_axis=1, tiled=True)  20.6 us
    all_to_all x1, waiting for transfers between devices, body(): lax.all_to_all(send_drive, 'dom', split_axis=1, concat_axis=1, tiled=True)  14.2 us
    all_to_all x1, waiting for transfers between devices, body(): lax.all_to_all(send_codes, 'dom', split_axis=1, concat_axis=1, tiled=True)  12.2 us
    all_to_all x1, waiting for transfers between devices, body(): lax.all_to_all(answer, 'dom', split_axis=1, concat_axis=1, tiled=True)  7.8 us
    unnamed x36, local copies, waits for them, and re-layouts  6.7 us
    all_to_all x1, starting transfers between devices, body(): lax.all_to_all(answer, 'dom', split_axis=1, concat_axis=1, tiled=True)  6.53 us
    all_to_all x1, starting transfers between devices, body(): lax.all_to_all(send_drive, 'dom', split_axis=1, concat_axis=1, tiled=True)  6.5 us
    ppermute x1, starting transfers between devices, padded_2(): after = lax.ppermute(leading, axis, down)  4.08 us
  transfers between devices with their start and end apart: 5, of which 3 were waited for; matrix products, arithmetic and copies ran while one was open for 3% of the time, Pallas kernels for 0%

commit v1 on v0

v1 whole, which is shorter than its diff:
```python
import functools

import jax
import jax.numpy as jnp
from jax import lax
from jax.experimental import pallas as pl
from jax.experimental.pallas import tpu as pltpu
from jax.sharding import PartitionSpec as P

MESH = pl.DeviceIdType.MESH
F32 = jnp.float32
BF16 = jnp.bfloat16
NY, NZ, NX = 4, 16, 4
NT = (((1,), (1,)), ((), ()))
TN = (((0,), (0,)), ((), ()))
NN = (((1,), (0,)), ((), ()))
OFFSETS = sorted(range(1, NZ), key=lambda d: min(d, NZ - d))


def mm(a, b, dims=NN):
    return lax.dot_general(a, b, dims, preferred_element_type=F32)


def iota(shape, axis):
    return lax.broadcasted_iota(jnp.int32, shape, axis)


def turn(x):
    return pltpu.roll(x, 64, 1)


def solve(points, codes, wbuf, skin):
    row, lane = iota((256, 128), 0), iota((256, 128), 1)
    half = lane // 64
    r2, c2 = iota((256, 256), 0), iota((256, 256), 1)
    order = ((r2 // 64) * 4 + ((r2 // 4) % 16) * 16 + r2 % 4 == c2).astype(BF16)
    x = mm(order, points)
    zsel = ((iota((256, 16), 0) // 4) % 16 == iota((256, 16), 1)).astype(BF16)
    spread = mm(zsel, codes.astype(BF16))
    spread = jnp.where(lane % 64 == (row // 64) * 4 + row % 4, spread, 0.0).astype(BF16)
    pick = (iota((128, 256), 0) // 64 == iota((128, 256), 1) // 128).astype(BF16)
    code2 = mm(spread, pick)
    xr = turn(x)
    total = skin[0]
    for k in range(1, 8):
        total = total + skin[k]
    sides = []
    for h in range(2):
        d2 = jnp.where(half == h, x, xr)
        code = code2[:, h * 128 : (h + 1) * 128]
        hi = (code < 0.0).astype(jnp.int32)
        bits = jnp.abs(code).astype(jnp.int32) - 1
        lo = jnp.bitwise_and(jnp.right_shift(bits, 7), 1)
        m = [jnp.bitwise_and(jnp.right_shift(bits, k), 1) == 1 for k in range(7)]
        both = [jnp.logical_and(m[k], m[k + 1]) for k in range(6)]
        alpha = sum(jnp.where(m[k], skin[k + 1], 0.0) for k in range(7))
        gamma = sum(jnp.where(m[k], skin[k], 0.0) for k in range(7))
        beta = sum(jnp.where(both[k], skin[k + 2], 0.0) for k in range(6))
        delta = sum(jnp.where(both[k], skin[k], 0.0) for k in range(6))
        sides.append((d2, hi == half, lo == half, alpha, beta, gamma, delta))

    def inverse(vs, h, rows):
        hi, lo = sides[h][1], sides[h][2]
        n = len(vs)
        masked = [jnp.where(hi, v, 0.0).astype(BF16) for v in vs]
        outs = [[] for _ in vs]
        for pair in range(4):
            part = slice(pair * 64, (pair + 1) * 64)
            stacked = masked[0][part] if n == 1 else jnp.concatenate([v[part] for v in masked], axis=0)
            got = mm(stacked, wbuf[h * 4 + pair, 0:128, :], NT)
            for i in range(n):
                outs[i].append(got[i * 64 : (i + 1) * 64])
        res = []
        for i in range(n):
            y = jnp.where(lo, jnp.concatenate(outs[i], axis=0), 0.0)
            res.append(y + turn(y))
        return res

    def couple(parts, h):
        n = len(parts)
        outs = [[] for _ in parts]
        for pair in range(4):
            part = slice(pair * 64, (pair + 1) * 64)
            c = wbuf[h * 4 + pair, 128:192, :]
            cc = jnp.concatenate([c, c], axis=0)
            stacked = parts[0][part] if n == 1 else jnp.concatenate([v[part] for v in parts], axis=0)
            got = mm(stacked, cc, NT)
            for i in range(n):
                outs[i].append(got[i * 64 : (i + 1) * 64])
        return [jnp.concatenate(o, axis=0) for o in outs]

    first = half == 0
    answers = []
    ys = [inverse([sides[h][0]], h, 64)[0] for h in range(2)]
    uvs = [
        couple([jnp.where(first, ys[h], 0.0).astype(BF16), jnp.where(first, 0.0, ys[h]).astype(BF16)], h)
        for h in range(2)
    ]
    pqs = [inverse(uvs[h], h, 128) for h in range(2)]
    for h in range(2):
        d2, _, _, alpha, beta, gamma, delta = sides[h]
        y, (p, q) = ys[h], pqs[h]
        up = alpha * y - beta * p - gamma * q
        down = gamma * y - alpha * p - delta * q
        z = total * d2 - couple([jnp.where(first, up, down).astype(BF16)], h)[0]
        high = z.astype(BF16).astype(F32)
        a, b = inverse([high, z - high], h, 128)
        answers.append((a + b) * 0.125)
    packed = jnp.where(first, answers[0], answers[1]).astype(BF16)
    return mm(order, packed, TN).astype(BF16)


def kernel(
    pot_hbm, types_hbm, sat_hbm, pat_hbm, inv_hbm, cpl_hbm, skin_hbm, out_ref,
    pot, typ, sat, pat, inv, cpl, skin, place, wbuf, send, recv, bsend, brecv, csend, crecv, hsend, hrecv,
    load_sem, ready, ps, pr, cs, cr, bs, br, ws, wr, hs, hr,
):
    dom, x = lax.axis_index("dom"), lax.axis_index("cell")
    c, z, y = lax.rem(dom, 2), lax.rem(dom // 2, NZ), dom // (2 * NZ)

    def at(yy, zz, cc):
        return ((yy * NZ + zz) * 2 + cc, x)

    zpeer = {d: at(y, lax.rem(z + d, NZ), c) for d in OFFSETS}
    zback = {d: at(y, lax.rem(z + NZ - d, NZ), c) for d in OFFSETS}
    wpeer = {h * 4 + u: at(lax.rem(y + NY - u, NY), z, c if h == 0 else 1 - c) for h in range(2) for u in range(NY)}
    wpeer.pop(0)
    index = dom * NX + x
    last = 2 * NY * NZ * NX - 1
    after = ((index + 1) // NX, lax.rem(index + 1, NX))
    before = ((index - 1 + NX) // NX - 1, lax.rem(index - 1 + NX, NX))
    has_after, has_before = index < last, index > 0

    barrier = pltpu.get_barrier_semaphore()
    for d in OFFSETS:
        @pl.when(z + d < NZ)
        def _(d=d):
            pl.semaphore_signal(barrier, inc=1, device_id=zpeer[d], device_id_type=MESH)
    for k in wpeer:
        pl.semaphore_signal(barrier, inc=1, device_id=wpeer[k], device_id_type=MESH)

    @pl.when(has_after)
    def _():
        pl.semaphore_signal(barrier, inc=1, device_id=after, device_id_type=MESH)

    @pl.when(has_before)
    def _():
        pl.semaphore_signal(barrier, inc=1, device_id=before, device_id_type=MESH)

    loads = [
        pltpu.make_async_copy(src, dst, load_sem.at[i])
        for i, (src, dst) in enumerate([
            (types_hbm, typ), (sat_hbm, sat), (pat_hbm, pat), (pot_hbm, pot), (inv_hbm, inv), (cpl_hbm, cpl),
            (skin_hbm, skin),
        ])
    ]
    for load in loads:
        load.start()
    pl.semaphore_wait(
        barrier, len(wpeer) + z + has_after.astype(jnp.int32) + has_before.astype(jnp.int32)
    )
    for d in OFFSETS:
        @pl.when(z - d >= 0)
        def _(d=d):
            pl.semaphore_signal(ready.at[d], inc=1, device_id=zback[d], device_id_type=MESH)
    for load in loads:
        load.wait()

    w = inv[...]
    wbuf[0, 0:128, :] = jnp.concatenate([w[0:128].astype(F32), w[128:256].astype(F32)], axis=1).astype(BF16)
    couple = cpl[...].astype(F32)
    wbuf[0, 128:192, :] = jnp.concatenate([couple, couple.T], axis=1).astype(BF16)
    sends = []
    for k in wpeer:
        copy = pltpu.make_async_remote_copy(
            wbuf.at[0], wbuf.at[k], ws.at[k], wr.at[k], device_id=wpeer[k], device_id_type=MESH
        )
        copy.start()
        sends.append(copy)
    weights = list(sends)

    field = pot[...]
    eye = iota((64, 128), 0) == iota((64, 128), 1)
    hsend[0] = jnp.sum(jnp.where(eye, field[:, 255:256], 0.0), axis=0, keepdims=True)
    hsend[1] = jnp.sum(jnp.where(eye, field[:, 0:1], 0.0), axis=0, keepdims=True)
    to_after = pltpu.make_async_remote_copy(
        hsend.at[0], hrecv.at[0], hs.at[0], hr.at[0], device_id=after, device_id_type=MESH
    )
    to_before = pltpu.make_async_remote_copy(
        hsend.at[1], hrecv.at[1], hs.at[1], hr.at[1], device_id=before, device_id_type=MESH
    )
    pl.when(has_after)(to_after.start)
    pl.when(has_before)(to_before.start)

    t = typ[...]
    onehot = (iota((128, 256), 0) == t).astype(BF16)
    earlier = (iota((256, 256), 0) < iota((256, 256), 1)).astype(BF16)
    rank = jnp.sum(onehot.astype(F32) * mm(onehot, earlier), axis=0, keepdims=True).astype(jnp.int32)
    t_y, t_z, t_c = t // (2 * NZ), (t // 2) % NZ, t % 2
    row = ((t_z - z + NZ) % NZ) * 16 + ((t_y - y + NY) % NY) * 4 + rank
    side = (t_c - c + 2) % 2
    both = jnp.concatenate([jnp.where(side == 0, row, -1), jnp.where(side == 1, row, -1)], axis=1)
    place[...] = (iota((256, 512), 0) == both).astype(BF16)
    level, bits = sat[...], pat[...]
    code = (1 + (level % 2) * 128 + bits) * jnp.where(level >= 2, -1, 1)
    code = jnp.broadcast_to(code.astype(F32), (64, 256)).astype(BF16)
    drive = field.astype(BF16)
    none = jnp.zeros((64, 256), BF16)
    table = jnp.concatenate(
        [jnp.concatenate([a, none], axis=1) if i == 0 else jnp.concatenate([none, a], axis=1)
         for a in (drive, code) for i in range(2)], axis=0
    )
    placed = mm(place[...], table, NT)
    points = placed[:, 0:128].astype(BF16).reshape(NZ, 16, 128)
    keep = iota((NZ, 16, 128), 2) % 64 == iota((NZ, 16, 128), 1)
    codes = jnp.sum(jnp.where(keep, placed[:, 128:256].reshape(NZ, 16, 128), 0.0), axis=1, keepdims=True)
    send[...] = points
    csend[...] = codes
    recv[0] = points[0]
    crecv[0] = codes[0]

    out, back = {}, {}
    for d in OFFSETS:
        out[d] = [
            pltpu.make_async_remote_copy(
                csend.at[d], crecv.at[d], cs.at[d], cr.at[d], device_id=zpeer[d], device_id_type=MESH
            ),
            pltpu.make_async_remote_copy(
                send.at[d], recv.at[d], ps.at[d], pr.at[d], device_id=zpeer[d], device_id_type=MESH
            ),
        ]
        back[d] = pltpu.make_async_remote_copy(
            bsend.at[d], brecv.at[d], bs.at[d], br.at[d], device_id=zback[d], device_id_type=MESH
        )

    for d in OFFSETS:
        @pl.when(z + d < NZ)
        def _(d=d):
            pl.semaphore_wait(ready.at[d], 1)
        for copy in out[d]:
            copy.start()

    pl.when(has_before)(to_after.wait_recv)
    pl.when(has_after)(to_before.wait_recv)
    lane = iota((64, 256), 1)
    wide = iota((64, 128), 0) == iota((64, 128), 1)
    left = jnp.sum(jnp.where(jnp.logical_and(wide, has_before), hrecv[0], 0.0), axis=1, keepdims=True)
    right = jnp.sum(jnp.where(jnp.logical_and(wide, has_after), hrecv[1], 0.0), axis=1, keepdims=True)
    left = jnp.where(lane == 0, left, pltpu.roll(field, 1, 1))
    right = jnp.where(lane == 255, right, pltpu.roll(field, 255, 1))
    pot[...] = field + 0.25 * (left - 2.0 * field + right)

    for copy in weights:
        copy.wait_recv()
    for d in OFFSETS:
        for copy in out[d]:
            copy.wait_recv()
    answer = solve(recv[...].reshape(256, 128), crecv[...].reshape(NZ, 128), wbuf, skin)
    bsend[...] = answer.reshape(NZ, 16, 128)
    for d in reversed(OFFSETS):
        back[d].start()
    brecv[0] = bsend[0]
    for d in OFFSETS:
        back[d].wait_recv()
    got = mm(brecv[...].reshape(256, 128), place[...], TN)
    out_ref[...] = pot[...] - (got[0:64, 0:256] + got[64:128, 256:512])

    for copy in sends:
        copy.wait_send()
    for d in OFFSETS:
        for copy in out[d]:
            copy.wait_send()
        back[d].wait_send()
    pl.when(has_after)(to_after.wait_send)
    pl.when(has_before)(to_before.wait_send)


def body(potential, types, saturation, pattern, inverses, coupling, skin):
    dma = pltpu.SemaphoreType.DMA
    return pl.pallas_call(
        kernel,
        out_shape=jax.ShapeDtypeStruct((64, 256), F32),
        in_specs=[pl.BlockSpec(memory_space=pl.ANY)] * 7,
        out_specs=pl.BlockSpec(memory_space=pltpu.VMEM),
        scratch_shapes=[
            pltpu.VMEM((64, 256), F32),
            pltpu.VMEM((1, 256), jnp.int32),
            pltpu.VMEM((1, 256), jnp.int32),
            pltpu.VMEM((1, 256), jnp.int32),
            pltpu.VMEM((256, 64), BF16),
            pltpu.VMEM((64, 64), BF16),
            pltpu.SMEM((8,), F32),
            pltpu.VMEM((256, 512), BF16),
            pltpu.VMEM((8, 192, 128), BF16),
            pltpu.VMEM((NZ, 16, 128), BF16),
            pltpu.VMEM((NZ, 16, 128), BF16),
            pltpu.VMEM((NZ, 16, 128), BF16),
            pltpu.VMEM((NZ, 16, 128), BF16),
            pltpu.VMEM((NZ, 1, 128), F32),
            pltpu.VMEM((NZ, 1, 128), F32),
            pltpu.VMEM((2, 1, 128), F32),
            pltpu.VMEM((2, 1, 128), F32),
            dma((7,)),
            pltpu.SemaphoreType.REGULAR((NZ,)),
            *[dma((NZ,)) for _ in range(6)],
            *[dma((8,)) for _ in range(2)],
            *[dma((2,)) for _ in range(2)],
        ],
        compiler_params=pltpu.CompilerParams(
            collective_id=0, has_side_effects=True, vmem_limit_bytes=32 * 1024 * 1024
        ),
        name="regroup_solve",
    )(
        potential,
        types.reshape(1, 256),
        saturation.reshape(1, 256),
        pattern.reshape(1, 256),
        inverses.reshape(256, 64),
        coupling.reshape(64, 64),
        skin,
    )


def solution(mesh):
    placed = (
        P(None, ("dom", "cell")),
        P(("dom", "cell"), None),
        P(("dom", "cell")),
        P(("dom", "cell")),
        P("dom", None, None, None),
        P("dom", None, None),
        P(),
    )
    return jax.shard_map(
        body, mesh=mesh, in_specs=placed, out_specs=P(None, ("dom", "cell")), check_vma=False
    )
```

time: 94.2 us -> 39.5 us (0.42)
  the two profiles are of different devices: /device:TPU:1 before, /device:TPU:6 now
where the time goes in v1:
time: 39.5 us; the launch traced here: 39.2 us
  Pallas kernels  35.4 us (90%)
  local copies, waits for them, and re-layouts  3.73 us (9%)
    pallas_call x1, Pallas kernels, body(): pl.pallas_call(kernel, out_shape=jax.ShapeDtypeStruct((64, 256), F32), in...  35.4 us
    unnamed x15, local copies, waits for them, and re-layouts  3.73 us

profile of v1, /device:TPU:6, one launch (start us, length us, event | category | flops | bytes accessed | tf_op | source)
XLA Modules:
  0.0 39.2 jit_solution(5068056548674158986)
XLA Ops:
  0.0 0.0 copy-start.4
  0.0 0.0 copy-start.5
  0.0 0.0 copy-start.3
  0.0 0.0 copy-start.6
  0.0 0.7 %copy-done.4 = s32[256]{0:T(256)S(1)} copy-done((s32[256]{0:T(256)S(1)}, s32[256]{0:T(256)}, u32[]{:S(2)}) %copy-start.4) | copy-done | bytes 1048
  0.7 0.0 copy-done.5
  0.7 0.0 copy-done.3
  0.7 0.0 copy-done.6
  0.7 0.0 copy-start
  0.7 0.8 %copy-done = f32[64,256]{1,0:T(8,128)S(1)} copy-done((f32[64,256]{1,0:T(8,128)S(1)}, f32[64,256]{1,0:T(8,128)}, u32[]{:S(2)}) %copy-start) | copy-done | bytes 65560
  1.6 0.0 copy-start.1
  1.6 0.8 %copy-done.1 = bf16[1,4,64,64]{3,2,1,0:T(8,128)(2,1)S(1)} copy-done((bf16[1,4,64,64]{3,2,1,0:T(8,128)(2,1)S(1)}, bf16[1,4,64,64]{3,2,1,0:T(8,128)(2,1)}, u32[]{:S(2)}) %copy-start.1) | copy-done | bytes 32792
  2.4 0.0 copy-start.2
  2.4 0.7 %copy-done.2 = bf16[1,64,64]{2,1,0:T(8,128)(2,1)S(1)} copy-done((bf16[1,64,64]{2,1,0:T(8,128)(2,1)S(1)}, bf16[1,64,64]{2,1,0:T(8,128)(2,1)}, u32[]{:S(2)}) %copy-start.2) | copy-done | bytes 8216
  3.1 35.4 %regroup_solve.1 = f32[64,256]{1,0:T(8,128)S(1)} custom-call(f32[64,256]{1,0:T(8,128)S(1)} %copy-done, s32[1,256]{1,0:T(1,128)S(1)} %bitcast.7, s32[1,256]{1,0:T(1,128)S(1)} %bitcast.8, s32[1,256]{1,0:T(1,128)S(1)} %bitcast.9, bf16[256,64]{1,0:T(8,128)(2,1)S(1)} %bitcast.5, bf16[64,64]{1,0:T(8,128)(2,1)S(1)} %bitcast.6, f32[8]{0:T(128)S(1)} %copy-done.6), custom_call_target="tpu_custom_call" | custom-call | tf_op jit(solution)/shard_map/regroup_solve/pallas_call | solution.py:280
  38.6 0.6 %copy.9 = f32[64,256]{1,0:T(8,128)} copy(f32[64,256]{1,0:T(8,128)S(1)} %regroup_solve.1) | data formatting | bytes 131072
Async XLA Ops:
  0.0 0.7 %copy-start.4 = (s32[256]{0:T(256)S(1)}, s32[256]{0:T(256)}, u32[]{:S(2)}) copy-start(s32[256]{0:T(256)} %param.9) | copy-start | bytes 3076
  0.0 0.7 %copy-start.5 = (s32[256]{0:T(256)S(1)}, s32[256]{0:T(256)}, u32[]{:S(2)}) copy-start(s32[256]{0:T(256)} %param.10) | copy-start | bytes 3076
  0.0 0.7 %copy-start.3 = (s32[256,1]{0,1:T(1,128)S(1)}, s32[256,1]{0,1:T(1,128)}, u32[]{:S(2)}) copy-start(s32[256,1]{0,1:T(1,128)} %param.8) | copy-start | bytes 3076
  0.0 0.7 %copy-start.6 = (f32[8]{0:T(128)S(1)}, f32[8]{0:T(128)}, u32[]{:S(2)}) copy-start(f32[8]{0:T(128)} %skin_hbm.1) | copy-start | bytes 100
  0.7 0.8 %copy-start = (f32[64,256]{1,0:T(8,128)S(1)}, f32[64,256]{1,0:T(8,128)}, u32[]{:S(2)}) copy-start(f32[64,256]{1,0:T(8,128)} %pot_hbm.1) | copy-start | bytes 196612
  1.6 0.8 %copy-start.1 = (bf16[1,4,64,64]{3,2,1,0:T(8,128)(2,1)S(1)}, bf16[1,4,64,64]{3,2,1,0:T(8,128)(2,1)}, u32[]{:S(2)}) copy-start(bf16[1,4,64,64]{3,2,1,0:T(8,128)(2,1)} %param.11) | copy-start | bytes 98308
  2.4 0.7 %copy-start.2 = (bf16[1,64,64]{2,1,0:T(8,128)(2,1)S(1)}, bf16[1,64,64]{2,1,0:T(8,128)(2,1)}, u32[]{:S(2)}) copy-start(bf16[1,64,64]{2,1,0:T(8,128)(2,1)} %param.12) | copy-start | bytes 24580

commit v2 on v1

v2 whole, which is shorter than its diff:
```python
import functools

import jax
import jax.numpy as jnp
from jax import lax
from jax.experimental import pallas as pl
from jax.experimental.pallas import tpu as pltpu
from jax.sharding import PartitionSpec as P

MESH = pl.DeviceIdType.MESH
F32 = jnp.float32
BF16 = jnp.bfloat16
NY, NZ, NX = 4, 16, 4
NT = (((1,), (1,)), ((), ()))
TN = (((0,), (0,)), ((), ()))
NN = (((1,), (0,)), ((), ()))
OFFSETS = sorted(range(1, NZ), key=lambda d: min(d, NZ - d))


def mm(a, b, dims=NN):
    return lax.dot_general(a, b, dims, preferred_element_type=F32)


def iota(shape, axis):
    return lax.broadcasted_iota(jnp.int32, shape, axis)


def turn(x):
    return pltpu.roll(x, 64, 1)


def coefficients(skin):
    row, lane = iota((128, 128), 0), iota((128, 128), 1)
    place_in = row % 64
    bit, part, first = place_in % 13, place_in // 13, lane < 64

    def chosen(lower, upper):
        value = jnp.zeros((128, 128), F32)
        for i in range(13):
            a = skin[lower[i]] if i in lower else 0.0
            b = skin[upper[i]] if i in upper else 0.0
            value = jnp.where(bit == i, jnp.where(first, a, b), value)
        return value

    above, here = {i: i + 1 for i in range(7)}, {i: i for i in range(7)}
    above2, here2 = {7 + i: i + 2 for i in range(6)}, {7 + i: i for i in range(6)}
    value = jnp.concatenate([chosen(above, here), chosen(above2, above), chosen(here, here2)], axis=1)
    row, part = iota((128, 384), 0), (iota((128, 384), 0) % 64) // 13
    high = value.astype(BF16).astype(F32)
    rest = value - high
    middle = rest.astype(BF16).astype(F32)
    value = jnp.where(part == 0, high, jnp.where(part == 1, middle, jnp.where(part == 2, rest - middle, 0.0)))
    return jnp.concatenate([jnp.where(row // 64 == h, value, 0.0) for h in range(2)], axis=1).astype(BF16)


def solve(points, codes, wbuf, table, total):
    n = codes.shape[0]
    rows, each = 16 * n, 4 * n
    row, lane = iota((rows, 128), 0), iota((rows, 128), 1)
    first = lane < 64
    r2, c2 = iota((rows, rows), 0), iota((rows, rows), 1)
    order = ((r2 // each) * 4 + ((r2 // 4) % n) * 16 + r2 % 4 == c2).astype(BF16)
    zsel = ((iota((rows, n), 0) // 4) % n == iota((rows, n), 1)).astype(BF16)
    spread = mm(zsel, codes.astype(BF16))
    x = mm(order, points)
    spread = jnp.where(lane % 64 == (row // each) * 4 + row % 4, spread, 0.0).astype(BF16)
    from_half, to = iota((128, 384), 0) // 64, iota((128, 384), 1)
    pick = (from_half == jnp.where(to < 256, to // 128, (to // 64) % 2)).astype(BF16)
    code = mm(spread, pick)
    bits = jnp.abs(code[:, 256:384]).astype(jnp.int32) - 1
    bit = (lane % 64) % 13
    mask = jnp.where(bit < 7, jnp.left_shift(1, bit), jnp.left_shift(3, jnp.maximum(bit - 7, 0)))
    held = jnp.logical_and(jnp.bitwise_and(bits, mask) == mask, lane % 64 < 39)
    factors = mm(held.astype(F32).astype(BF16), table)
    xr = turn(x)
    sides = []
    for h in range(2):
        d2 = jnp.where(first, x, xr) if h == 0 else jnp.where(first, xr, x)
        c = code[:, h * 128 : (h + 1) * 128]
        hi = jnp.where(first, c, -c) >= 0.0
        lo = (jnp.abs(c) > 128.0) != first
        sides.append((d2, hi, lo))

    def inverse(vs, h):
        _, hi, lo = sides[h]
        masked = [jnp.where(hi, v, 0.0).astype(BF16) for v in vs]
        outs = [[] for _ in vs]
        for pair in range(4):
            part = slice(pair * each, (pair + 1) * each)
            stacked = masked[0][part] if len(vs) == 1 else jnp.concatenate([v[part] for v in masked], axis=0)
            got = mm(stacked, wbuf[h * 4 + pair, 0:128, :], NT)
            for i in range(len(vs)):
                outs[i].append(got[i * each : (i + 1) * each])
        res = []
        for out in outs:
            y = jnp.where(lo, jnp.concatenate(out, axis=0), 0.0)
            res.append(y + turn(y))
        return res

    def couple(parts, h):
        outs = [[] for _ in parts]
        for pair in range(4):
            part = slice(pair * each, (pair + 1) * each)
            c = wbuf[h * 4 + pair, 128:192, :]
            stacked = parts[0][part] if len(parts) == 1 else jnp.concatenate([v[part] for v in parts], axis=0)
            got = mm(stacked, jnp.concatenate([c, c], axis=0), NT)
            for i in range(len(parts)):
                outs[i].append(got[i * each : (i + 1) * each])
        return [jnp.concatenate(o, axis=0) for o in outs]

    ys = [inverse([sides[h][0]], h)[0] for h in range(2)]
    uvs = [
        couple([jnp.where(first, ys[h], 0.0).astype(BF16), jnp.where(first, 0.0, ys[h]).astype(BF16)], h)
        for h in range(2)
    ]
    pqs = [inverse(uvs[h], h) for h in range(2)]
    answers = []
    for h in range(2):
        f = [factors[:, h * 384 + i * 128 : h * 384 + (i + 1) * 128] for i in range(3)]
        mixed = f[0] * ys[h] - f[1] * pqs[h][0] - f[2] * pqs[h][1]
        z = total * sides[h][0] - couple([mixed.astype(BF16)], h)[0]
        high = z.astype(BF16).astype(F32)
        a, b = inverse([high, z - high], h)
        answers.append((a + b) * 0.125)
    packed = jnp.where(first, answers[0], answers[1]).astype(BF16)
    return mm(order, packed, TN).astype(BF16)


def kernel(
    pot_hbm, types_hbm, sat_hbm, pat_hbm, inv_hbm, cpl_hbm, skin_hbm, out_ref,
    pot, typ, sat, pat, inv, cpl, skin, place, table, wbuf, send, recv, bsend, brecv, csend, crecv, hsend, hrecv,
    load_sem, ready, wready, hready, ps, pr, cs, cr, bs, br, ws, wr, hs, hr,
):
    dom, x = lax.axis_index("dom"), lax.axis_index("cell")
    c, z, y = lax.rem(dom, 2), lax.rem(dom // 2, NZ), dom // (2 * NZ)

    def at(yy, zz, cc):
        return ((yy * NZ + zz) * 2 + cc, x)

    ahead = {d: lax.rem(z + d, NZ) for d in OFFSETS}
    behind = {d: lax.rem(z + NZ - d, NZ) for d in OFFSETS}
    zpeer = {d: at(y, ahead[d], c) for d in OFFSETS}
    zback = {d: at(y, behind[d], c) for d in OFFSETS}
    wpeer, later = {}, {}
    key = y * 2 + 1 - c
    for k in range(1, 8):
        yy, cc = lax.rem(y + NY - k % 4, NY), c if k < 4 else 1 - c
        wpeer[k] = at(yy, z, cc)
        later[k] = yy * 2 + 1 - cc > key
    index = dom * NX + x
    after = ((index + 1) // NX, lax.rem(index + 1, NX))
    before = ((index - 1 + NX) // NX - 1, lax.rem(index - 1 + NX, NX))
    has_after, has_before = index < 2 * NY * NZ * NX - 1, index > 0

    def follows(xx, cc, zz):
        return jnp.logical_or(xx < NX - 1, jnp.logical_and(cc == 1, zz < NZ - 1))

    back_dom = before[0]
    i_first = jnp.logical_and(has_after, follows(x, c, z))
    i_last = jnp.logical_and(has_after, jnp.logical_not(follows(x, c, z)))
    b_follows = follows(before[1], lax.rem(back_dom, 2), lax.rem(back_dom // 2, NZ))
    b_first = jnp.logical_and(has_before, b_follows)
    b_last = jnp.logical_and(has_before, jnp.logical_not(b_follows))

    barrier = pltpu.get_barrier_semaphore()
    for d in OFFSETS:
        @pl.when(z + d < NZ)
        def _(d=d):
            pl.semaphore_signal(barrier, inc=1, device_id=zpeer[d], device_id_type=MESH)
    for k in wpeer:
        @pl.when(later[k])
        def _(k=k):
            pl.semaphore_signal(barrier, inc=1, device_id=wpeer[k], device_id_type=MESH)

    @pl.when(i_first)
    def _():
        pl.semaphore_signal(barrier, inc=1, device_id=after, device_id_type=MESH)

    @pl.when(b_last)
    def _():
        pl.semaphore_signal(barrier, inc=1, device_id=before, device_id_type=MESH)

    loads = [
        pltpu.make_async_copy(src, dst, load_sem.at[i])
        for i, (src, dst) in enumerate([
            (types_hbm, typ), (sat_hbm, sat), (pat_hbm, pat), (pot_hbm, pot), (inv_hbm, inv), (cpl_hbm, cpl),
            (skin_hbm, skin),
        ])
    ]
    for load in loads:
        load.start()
    n_earlier = key + z + b_first.astype(jnp.int32) + i_last.astype(jnp.int32)

    @pl.when(n_earlier > 0)
    def _():
        pl.semaphore_wait(barrier, n_earlier)

    for d in reversed(OFFSETS):
        @pl.when(z - d >= 0)
        def _(d=d):
            pl.semaphore_signal(ready.at[d], inc=1, device_id=zback[d], device_id_type=MESH)
    for k in wpeer:
        @pl.when(jnp.logical_not(later[k]))
        def _(k=k):
            at_peer = k // 4 * 4 + (4 - k % 4) % 4
            pl.semaphore_signal(wready.at[at_peer], inc=1, device_id=wpeer[k], device_id_type=MESH)

    @pl.when(i_last)
    def _():
        pl.semaphore_signal(hready.at[1], inc=1, device_id=after, device_id_type=MESH)

    @pl.when(b_first)
    def _():
        pl.semaphore_signal(hready.at[0], inc=1, device_id=before, device_id_type=MESH)

    for load in loads:
        load.wait()

    field = pot[...]
    t = typ[...]
    onehot = (iota((128, 256), 0) == t).astype(BF16)
    earlier = (iota((256, 256), 0) < iota((256, 256), 1)).astype(BF16)
    rank = jnp.sum(onehot.astype(F32) * mm(onehot, earlier), axis=0, keepdims=True).astype(jnp.int32)
    t_y, t_z, t_c = t // (2 * NZ), (t // 2) % NZ, t % 2
    row = t_z * 16 + ((t_y - y + NY) % NY) * 4 + rank
    side = (t_c - c + 2) % 2
    both = jnp.concatenate([jnp.where(side == 0, row, -1), jnp.where(side == 1, row, -1)], axis=1)
    place[...] = (iota((256, 512), 0) == both).astype(BF16)
    level, bits = sat[...], pat[...]
    code = (1 + (level % 2) * 128 + bits) * jnp.where(level >= 2, -1, 1)
    code = jnp.broadcast_to(code.astype(F32), (64, 256)).astype(BF16)
    drive = field.astype(BF16)
    none = jnp.zeros((64, 256), BF16)
    spread = jnp.concatenate(
        [jnp.concatenate([a, none], axis=1) if i == 0 else jnp.concatenate([none, a], axis=1)
         for a in (drive, code) for i in range(2)], axis=0
    )
    placed = mm(place[...], spread, NT)
    keep = iota((NZ, 16, 128), 2) % 64 == iota((NZ, 16, 128), 1)
    send[...] = placed[:, 0:128].astype(BF16).reshape(NZ, 16, 128)
    csend[...] = jnp.sum(jnp.where(keep, placed[:, 128:256].reshape(NZ, 16, 128), 0.0), axis=1, keepdims=True)

    out, back, backin = {}, {}, {}
    for d in OFFSETS:
        out[d] = [
            pltpu.make_async_remote_copy(
                csend.at[ahead[d]], crecv.at[z], cs.at[d], cr.at[d], device_id=zpeer[d], device_id_type=MESH
            ),
            pltpu.make_async_remote_copy(
                send.at[ahead[d]], recv.at[z], ps.at[d], pr.at[d], device_id=zpeer[d], device_id_type=MESH
            ),
        ]
        back[d] = pltpu.make_async_remote_copy(
            bsend.at[behind[d]], brecv.at[z], bs.at[d], br.at[d], device_id=zback[d], device_id_type=MESH
        )
    for d in OFFSETS:
        @pl.when(z + d >= NZ)
        def _(d=d):
            for copy in out[d]:
                copy.start()

    w = inv[...]
    wbuf[0, 0:128, :] = jnp.concatenate([w[0:128].astype(F32), w[128:256].astype(F32)], axis=1).astype(BF16)
    block = cpl[...].astype(F32)
    wbuf[0, 128:192, :] = jnp.concatenate([block, block.T], axis=1).astype(BF16)
    weights = {
        k: pltpu.make_async_remote_copy(
            wbuf.at[0], wbuf.at[k], ws.at[k], wr.at[k], device_id=wpeer[k], device_id_type=MESH
        )
        for k in wpeer
    }
    for want in (False, True):
        for k in weights:
            @pl.when(later[k] == want)
            def _(k=k, want=want):
                if want:
                    pl.semaphore_wait(wready.at[k], 1)
                weights[k].start()

    eye = iota((64, 128), 0) == iota((64, 128), 1)
    hsend[0] = jnp.sum(jnp.where(eye, field[:, 255:256], 0.0), axis=0, keepdims=True)
    hsend[1] = jnp.sum(jnp.where(eye, field[:, 0:1], 0.0), axis=0, keepdims=True)
    to_after = pltpu.make_async_remote_copy(
        hsend.at[0], hrecv.at[0], hs.at[0], hr.at[0], device_id=after, device_id_type=MESH
    )
    to_before = pltpu.make_async_remote_copy(
        hsend.at[1], hrecv.at[1], hs.at[1], hr.at[1], device_id=before, device_id_type=MESH
    )

    @pl.when(i_first)
    def _():
        pl.semaphore_wait(hready.at[0], 1)

    @pl.when(b_last)
    def _():
        pl.semaphore_wait(hready.at[1], 1)

    pl.when(has_after)(to_after.start)
    pl.when(has_before)(to_before.start)

    for d in OFFSETS:
        @pl.when(z + d < NZ)
        def _(d=d):
            pl.semaphore_wait(ready.at[d], 1)
            for copy in out[d]:
                copy.start()
    recv[z] = send[z]
    crecv[z] = csend[z]

    table[...] = coefficients(skin)
    total = skin[0]
    for k in range(1, 8):
        total = total + skin[k]

    for k in weights:
        weights[k].wait_recv()
    for d in OFFSETS:
        for copy in out[d]:
            copy.wait_recv()
    answer = solve(recv[...].reshape(256, 128), crecv[...].reshape(NZ, 128), wbuf, table[...], total)
    bsend[...] = answer.reshape(NZ, 16, 128)
    for d in reversed(OFFSETS):
        back[d].start()
    brecv[z] = bsend[z]

    pl.when(has_before)(to_after.wait_recv)
    pl.when(has_after)(to_before.wait_recv)
    lane = iota((64, 256), 1)
    left = jnp.sum(jnp.where(jnp.logical_and(eye, has_before), hrecv[0], 0.0), axis=1, keepdims=True)
    right = jnp.sum(jnp.where(jnp.logical_and(eye, has_after), hrecv[1], 0.0), axis=1, keepdims=True)
    left = jnp.where(lane == 0, left, pltpu.roll(field, 1, 1))
    right = jnp.where(lane == 255, right, pltpu.roll(field, 255, 1))
    pot[...] = field + 0.25 * (left - 2.0 * field + right)

    for d in OFFSETS:
        back[d].wait_recv()
    got = mm(brecv[...].reshape(256, 128), place[...], TN)
    out_ref[...] = pot[...] - (got[0:64, 0:256] + got[64:128, 256:512])

    for k in weights:
        weights[k].wait_send()
    for d in OFFSETS:
        for copy in out[d]:
            copy.wait_send()
        back[d].wait_send()
    pl.when(has_after)(to_after.wait_send)
    pl.when(has_before)(to_before.wait_send)


def body(potential, types, saturation, pattern, inverses, coupling, skin):
    dma = pltpu.SemaphoreType.DMA
    return pl.pallas_call(
        kernel,
        out_shape=jax.ShapeDtypeStruct((64, 256), F32),
        in_specs=[pl.BlockSpec(memory_space=pl.ANY)] * 7,
        out_specs=pl.BlockSpec(memory_space=pltpu.VMEM),
        scratch_shapes=[
            pltpu.VMEM((64, 256), F32),
            pltpu.VMEM((1, 256), jnp.int32),
            pltpu.VMEM((1, 256), jnp.int32),
            pltpu.VMEM((1, 256), jnp.int32),
            pltpu.VMEM((256, 64), BF16),
            pltpu.VMEM((64, 64), BF16),
            pltpu.SMEM((8,), F32),
            pltpu.VMEM((256, 512), BF16),
            pltpu.VMEM((128, 768), BF16),
            pltpu.VMEM((8, 192, 128), BF16),
            pltpu.VMEM((NZ, 16, 128), BF16),
            pltpu.VMEM((NZ, 16, 128), BF16),
            pltpu.VMEM((NZ, 16, 128), BF16),
            pltpu.VMEM((NZ, 16, 128), BF16),
            pltpu.VMEM((NZ, 1, 128), F32),
            pltpu.VMEM((NZ, 1, 128), F32),
            pltpu.VMEM((2, 1, 128), F32),
            pltpu.VMEM((2, 1, 128), F32),
            dma((7,)),
            pltpu.SemaphoreType.REGULAR((NZ,)),
            pltpu.SemaphoreType.REGULAR((8,)),
            pltpu.SemaphoreType.REGULAR((2,)),
            *[dma((NZ,)) for _ in range(6)],
            *[dma((8,)) for _ in range(2)],
            *[dma((2,)) for _ in range(2)],
        ],
        compiler_params=pltpu.CompilerParams(
            collective_id=0, has_side_effects=True, vmem_limit_bytes=64 * 1024 * 1024
        ),
        name="regroup_solve",
    )(
        potential,
        types.reshape(1, 256),
        saturation.reshape(1, 256),
        pattern.reshape(1, 256),
        inverses.reshape(256, 64),
        coupling.reshape(64, 64),
        skin,
    )


def solution(mesh):
    placed = (
        P(None, ("dom", "cell")),
        P(("dom", "cell"), None),
        P(("dom", "cell")),
        P(("dom", "cell")),
        P("dom", None, None, None),
        P("dom", None, None),
        P(),
    )
    return jax.shard_map(
        body, mesh=mesh, in_specs=placed, out_specs=P(None, ("dom", "cell")), check_vma=False
    )
```

time: 39.5 us -> 37.5 us (0.949)
  the two profiles are of different devices: /device:TPU:6 before, /device:TPU:24 now
where the time goes in v2:
time: 37.5 us; the launch traced here: 37.3 us
  Pallas kernels  35.8 us (95%)
  local copies, waits for them, and re-layouts  1.47 us (4%)
    pallas_call x1, Pallas kernels, body(): pl.pallas_call(kernel, out_shape=jax.ShapeDtypeStruct((64, 256), F32), in...  35.8 us
    unnamed x1, local copies, waits for them, and re-layouts  1.47 us

profile of v2, /device:TPU:24, one launch (start us, length us, event | category | flops | bytes accessed | tf_op | source)
XLA Modules:
  0.0 37.3 jit_solution(17647267252101409965)
XLA Ops:
  0.0 35.8 %regroup_solve.1 = f32[64,256]{1,0:T(8,128)} custom-call(f32[64,256]{1,0:T(8,128)} %pot_hbm.1, s32[1,256]{1,0:T(1,128)} %bitcast.7, s32[1,256]{1,0:T(1,128)} %bitcast.8, s32[1,256]{1,0:T(1,128)} %bitcast.9, bf16[256,64]{1,0:T(8,128)(2,1)} %bitcast.5, bf16[64,64]{1,0:T(8,128)(2,1)} %bitcast.6, f32[8]{0:T(128)} %skin_hbm.1), custom_call_target="tpu_custom_call" | custom-call | tf_op jit(solution)/shard_map/regroup_solve/pallas_call | solution.py:352
  35.8 1.5 %copy.9 = f32[64,256]{1,0:T(8,128)} copy(f32[64,256]{1,0:T(8,128)} %regroup_solve.1) | data formatting | bytes 131072

commit v3 on v2

--- a/solution.py
+++ b/solution.py
@@ -14,6 +14,8 @@
 NT = (((1,), (1,)), ((), ()))
 TN = (((0,), (0,)), ((), ()))
 NN = (((1,), (0,)), ((), ()))
+GROUP = 4
+FAR = range(GROUP + 1, 2 * GROUP + 2)
 OFFSETS = sorted(range(1, NZ), key=lambda d: min(d, NZ - d))
 
 
@@ -128,8 +130,8 @@
 
 def kernel(
     pot_hbm, types_hbm, sat_hbm, pat_hbm, inv_hbm, cpl_hbm, skin_hbm, out_ref,
-    pot, typ, sat, pat, inv, cpl, skin, place, table, wbuf, send, recv, bsend, brecv, csend, crecv, hsend, hrecv,
-    load_sem, ready, wready, hready, ps, pr, cs, cr, bs, br, ws, wr, hs, hr,
+    pot, typ, sat, pat, inv, cpl, skin, place, table, wbuf, send, recv, bsend, brecv, csend, crecv, hsend, hrecv, rbuf, crbuf,
+    load_sem, ready, wready, hready, ps, pr, cs, cr, bs, br, ws, wr, hs, hr, bds, bdr, fs, cfs,
 ):
     dom, x = lax.axis_index("dom"), lax.axis_index("cell")
     c, z, y = lax.rem(dom, 2), lax.rem(dom // 2, NZ), dom // (2 * NZ)
@@ -152,15 +154,12 @@
     before = ((index - 1 + NX) // NX - 1, lax.rem(index - 1 + NX, NX))
     has_after, has_before = index < 2 * NY * NZ * NX - 1, index > 0
 
-    def follows(xx, cc, zz):
-        return jnp.logical_or(xx < NX - 1, jnp.logical_and(cc == 1, zz < NZ - 1))
-
-    back_dom = before[0]
-    i_first = jnp.logical_and(has_after, follows(x, c, z))
-    i_last = jnp.logical_and(has_after, jnp.logical_not(follows(x, c, z)))
-    b_follows = follows(before[1], lax.rem(back_dom, 2), lax.rem(back_dom // 2, NZ))
-    b_first = jnp.logical_and(has_before, b_follows)
-    b_last = jnp.logical_and(has_before, jnp.logical_not(b_follows))
+    i_first = jnp.logical_and(has_after, x < NX - 1)
+    i_last = jnp.logical_and(has_after, x == NX - 1)
+    b_first = jnp.logical_and(has_before, x > 0)
+    b_last = jnp.logical_and(has_before, x == 0)
+    relayed = z < GROUP
+    relays = jnp.logical_and(z >= GROUP, z < 2 * GROUP)
 
     barrier = pltpu.get_barrier_semaphore()
     for d in OFFSETS:
@@ -277,6 +276,54 @@
                     pl.semaphore_wait(wready.at[k], 1)
                 weights[k].start()
 
+    span = pl.ds(lax.rem(z + FAR[0], NZ - len(FAR) + 1), len(FAR))
+    bundle = [
+        pltpu.make_async_remote_copy(
+            src.at[span], dst, bds.at[i], bdr.at[i], device_id=zpeer[GROUP], device_id_type=MESH
+        )
+        for i, (src, dst) in enumerate([(csend, crbuf), (send, rbuf)])
+    ]
+    origin = jnp.maximum(z - GROUP, 0)
+    onward = {}
+    for j in range(1, len(FAR) + 1):
+        onward[j] = [
+            pltpu.make_async_remote_copy(
+                src.at[j - 1], dst.at[origin], ss.at[j - 1], rs.at[j + GROUP],
+                device_id=zpeer[j], device_id_type=MESH,
+            )
+            for src, dst, ss, rs in ((crbuf, crecv, cfs, cr), (rbuf, recv, fs, pr))
+        ]
+
+    def send_on(d):
+        higher = z + d < NZ
+
+        @pl.when(jnp.logical_and(higher, jnp.logical_not(relayed)) if d in FAR else higher)
+        def _():
+            pl.semaphore_wait(ready.at[d], 1)
+            for copy in out[d]:
+                copy.start()
+
+    for d in range(1, GROUP + 2):
+        send_on(d)
+        if d == GROUP:
+            @pl.when(relayed)
+            def _():
+                for copy in bundle:
+                    copy.start()
+
+    @pl.when(relays)
+    def _():
+        for copy in bundle:
+            copy.wait_recv()
+        for j in reversed(onward):
+            for copy in onward[j]:
+                copy.start()
+
+    for d in range(GROUP + 2, NZ):
+        send_on(d)
+    recv[z] = send[z]
+    crecv[z] = csend[z]
+
     eye = iota((64, 128), 0) == iota((64, 128), 1)
     hsend[0] = jnp.sum(jnp.where(eye, field[:, 255:256], 0.0), axis=0, keepdims=True)
     hsend[1] = jnp.sum(jnp.where(eye, field[:, 0:1], 0.0), axis=0, keepdims=True)
@@ -298,15 +345,6 @@
     pl.when(has_after)(to_after.start)
     pl.when(has_before)(to_before.start)
 
-    for d in OFFSETS:
-        @pl.when(z + d < NZ)
-        def _(d=d):
-            pl.semaphore_wait(ready.at[d], 1)
-            for copy in out[d]:
-                copy.start()
-    recv[z] = send[z]
-    crecv[z] = csend[z]
-
     table[...] = coefficients(skin)
     total = skin[0]
     for k in range(1, 8):
@@ -314,13 +352,22 @@
 
     for k in weights:
         weights[k].wait_recv()
-    for d in OFFSETS:
-        for copy in out[d]:
-            copy.wait_recv()
-    answer = solve(recv[...].reshape(256, 128), crecv[...].reshape(NZ, 128), wbuf, table[...], total)
-    bsend[...] = answer.reshape(NZ, 16, 128)
-    for d in reversed(OFFSETS):
-        back[d].start()
+    spreads = table[...]
+    for start, stop in ((0, GROUP), (GROUP, NZ)):
+        for d in OFFSETS:
+            @pl.when(jnp.logical_and(behind[d] >= start, behind[d] < stop))
+            def _(d=d):
+                for copy in out[d]:
+                    copy.wait_recv()
+        n = stop - start
+        answer = solve(
+            recv[start:stop].reshape(n * 16, 128), crecv[start:stop].reshape(n, 128), wbuf, spreads, total
+        )
+        bsend[start:stop] = answer.reshape(n, 16, 128)
+        for d in reversed(OFFSETS):
+            @pl.when(jnp.logical_and(behind[d] >= start, behind[d] < stop))
+            def _(d=d):
+                back[d].start()
     brecv[z] = bsend[z]
 
     pl.when(has_before)(to_after.wait_recv)
@@ -340,9 +387,31 @@
     for k in weights:
         weights[k].wait_send()
     for d in OFFSETS:
-        for copy in out[d]:
+        if d in FAR:
+            @pl.when(jnp.logical_not(relayed))
+            def _(d=d):
+                for copy in out[d]:
+                    copy.wait_send()
+
+            @pl.when(relayed)
+            def _(d=d):
+                pl.semaphore_wait(ready.at[d], 1)
+        else:
+            for copy in out[d]:
+                copy.wait_send()
+        back[d].wait_send()
+
+    @pl.when(relayed)
+    def _():
+        for copy in bundle:
             copy.wait_send()
-        back[d].wait_send()
+
+    @pl.when(relays)
+    def _():
+        for j in onward:
+            for copy in onward[j]:
+                copy.wait_send()
+
     pl.when(has_after)(to_after.wait_send)
     pl.when(has_before)(to_before.wait_send)
 
@@ -373,13 +442,16 @@
             pltpu.VMEM((NZ, 1, 128), F32),
             pltpu.VMEM((2, 1, 128), F32),
             pltpu.VMEM((2, 1, 128), F32),
+            pltpu.VMEM((len(FAR), 16, 128), BF16),
+            pltpu.VMEM((len(FAR), 1, 128), F32),
             dma((7,)),
             pltpu.SemaphoreType.REGULAR((NZ,)),
             pltpu.SemaphoreType.REGULAR((8,)),
             pltpu.SemaphoreType.REGULAR((2,)),
             *[dma((NZ,)) for _ in range(6)],
             *[dma((8,)) for _ in range(2)],
-            *[dma((2,)) for _ in range(2)],
+            *[dma((2,)) for _ in range(4)],
+            *[dma((len(FAR),)) for _ in range(2)],
         ],
         compiler_params=pltpu.CompilerParams(
             collective_id=0, has_side_effects=True, vmem_limit_bytes=64 * 1024 * 1024

time: 37.5 us -> 35.1 us (0.936)
  the two profiles are of different devices: /device:TPU:24 before, /device:TPU:32 now
where the time goes in v3:
time: 35.1 us; the launch traced here: 34.9 us
  Pallas kernels  33.4 us (95%)
  local copies, waits for them, and re-layouts  1.47 us (4%)
    pallas_call x1, Pallas kernels, body(): pl.pallas_call(kernel, out_shape=jax.ShapeDtypeStruct((64, 256), F32), in...  33.4 us
    unnamed x1, local copies, waits for them, and re-layouts  1.47 us

profile of v3, /device:TPU:32, one launch (start us, length us, event | category | flops | bytes accessed | tf_op | source)
XLA Modules:
  0.0 34.9 jit_solution(5231130929356236292)
XLA Ops:
  0.0 33.4 %regroup_solve.1 = f32[64,256]{1,0:T(8,128)} custom-call(f32[64,256]{1,0:T(8,128)} %pot_hbm.1, s32[1,256]{1,0:T(1,128)} %bitcast.7, s32[1,256]{1,0:T(1,128)} %bitcast.8, s32[1,256]{1,0:T(1,128)} %bitcast.9, bf16[256,64]{1,0:T(8,128)(2,1)} %bitcast.5, bf16[64,64]{1,0:T(8,128)(2,1)} %bitcast.6, f32[8]{0:T(128)} %skin_hbm.1), custom_call_target="tpu_custom_call" | custom-call | tf_op jit(solution)/shard_map/regroup_solve/pallas_call | solution.py:421
  33.5 1.5 %copy.9 = f32[64,256]{1,0:T(8,128)} copy(f32[64,256]{1,0:T(8,128)} %regroup_solve.1) | data formatting | bytes 131072

commit v4 on v3

v4 whole, which is shorter than its diff:
```python
import functools

import jax
import jax.numpy as jnp
from jax import lax
from jax.experimental import pallas as pl
from jax.experimental.pallas import tpu as pltpu
from jax.sharding import PartitionSpec as P

MESH = pl.DeviceIdType.MESH
F32 = jnp.float32
BF16 = jnp.bfloat16
NY, NZ, NX = 4, 16, 4
NT = (((1,), (1,)), ((), ()))
TN = (((0,), (0,)), ((), ()))
NN = (((1,), (0,)), ((), ()))
GROUP, HALF = 4, NZ // 2
FAR = range(GROUP + 1, 2 * GROUP + 2)
OFFSETS = sorted(range(1, NZ), key=lambda d: min(d, NZ - d))


def mm(a, b, dims=NN):
    return lax.dot_general(a, b, dims, preferred_element_type=F32)


def iota(shape, axis):
    return lax.broadcasted_iota(jnp.int32, shape, axis)


def turn(x):
    return pltpu.roll(x, 64, 1)


def coefficients(skin):
    row, lane = iota((128, 128), 0), iota((128, 128), 1)
    place_in = row % 64
    bit, part, first = place_in % 13, place_in // 13, lane < 64

    def chosen(lower, upper):
        value = jnp.zeros((128, 128), F32)
        for i in range(13):
            a = skin[lower[i]] if i in lower else 0.0
            b = skin[upper[i]] if i in upper else 0.0
            value = jnp.where(bit == i, jnp.where(first, a, b), value)
        return value

    above, here = {i: i + 1 for i in range(7)}, {i: i for i in range(7)}
    above2, here2 = {7 + i: i + 2 for i in range(6)}, {7 + i: i for i in range(6)}
    value = jnp.concatenate([chosen(above, here), chosen(above2, above), chosen(here, here2)], axis=1)
    row, part = iota((128, 384), 0), (iota((128, 384), 0) % 64) // 13
    high = value.astype(BF16).astype(F32)
    rest = value - high
    middle = rest.astype(BF16).astype(F32)
    value = jnp.where(part == 0, high, jnp.where(part == 1, middle, jnp.where(part == 2, rest - middle, 0.0)))
    return jnp.concatenate([jnp.where(row // 64 == h, value, 0.0) for h in range(2)], axis=1).astype(BF16)


def product(a, c):
    low = iota((128, 128), 1) < 64
    a = a.astype(F32)
    levels = jnp.concatenate([jnp.where(low, a, 0.0), jnp.where(low, 0.0, a)], axis=0).astype(BF16)
    return mm(levels, jnp.concatenate([c, c], axis=0)).astype(BF16)


def solve(points, codes, wbuf, gbuf, table, total):
    n = codes.shape[0]
    rows = 16 * n
    row, lane = iota((rows, 128), 0), iota((rows, 128), 1)
    first = lane < 64
    pair = (row // 4) % 4
    spread = jnp.broadcast_to(codes.reshape(n, 1, 128), (n, 16, 128)).reshape(rows, 128)
    spread = jnp.where(lane % 64 == row % 16, spread, 0.0).astype(BF16)
    from_half, to = iota((128, 384), 0) // 64, iota((128, 384), 1)
    pick = (from_half == jnp.where(to < 256, to // 128, (to // 64) % 2)).astype(BF16)
    code = mm(spread, pick)
    bits = jnp.abs(code[:, 256:384]).astype(jnp.int32) - 1
    bit = (lane % 64) % 13
    mask = jnp.where(bit < 7, jnp.left_shift(1, bit), jnp.left_shift(3, jnp.maximum(bit - 7, 0)))
    held = jnp.logical_and(jnp.bitwise_and(bits, mask) == mask, lane % 64 < 39)
    factors = mm(held.astype(F32).astype(BF16), table)
    x = points.astype(F32)
    xr = turn(x)

    def by_pair(v):
        return jnp.concatenate([jnp.where(pair == p, v, 0.0).astype(BF16) for p in range(4)], axis=1)

    def doubled(v, lo):
        v = jnp.where(lo, v, 0.0)
        return v + turn(v)

    sides, ys, pqs, answers = [], [], [], []
    for h in range(2):
        c = code[:, h * 128 : (h + 1) * 128]
        sides.append((c < 0.0, (jnp.abs(c) > 128.0) != first))
        upper = sides[h][0]
        d2 = jnp.where(first, x, xr) if h == 0 else jnp.where(first, xr, x)
        blocks = jnp.concatenate([wbuf[h * 4 + p, 0:128, :] for p in range(4)], axis=1)
        ys.append(doubled(mm(by_pair(jnp.where(upper != first, d2, 0.0)), blocks, NT), sides[h][1]))

    def coupled(v, h):
        return mm(v, jnp.concatenate([gbuf[h * 4 + p] for p in range(4)], axis=1), NT)

    for h in range(2):
        upper, lo = sides[h]
        y = ys[h]
        both = jnp.concatenate([by_pair(jnp.where(first, y, 0.0)), by_pair(jnp.where(first, 0.0, y))], axis=0)
        got = coupled(both, h)
        pqs.append([doubled(jnp.where(upper, g[:, 128:256], g[:, 0:128]), lo) for g in (got[:rows], got[rows:])])
    for h in range(2):
        upper, lo = sides[h]
        f = [factors[:, h * 384 + i * 128 : h * 384 + (i + 1) * 128] for i in range(3)]
        mixed = f[0] * ys[h] - f[1] * pqs[h][0] - f[2] * pqs[h][1]
        got = coupled(by_pair(mixed), h)
        rest = doubled(jnp.where(upper, got[:, 128:256], got[:, 0:128]), lo)
        answers.append((total * ys[h] - rest) * 0.125)
    return jnp.where(first, answers[0], answers[1]).astype(BF16)


def kernel(
    pot_hbm, types_hbm, sat_hbm, pat_hbm, inv_hbm, cpl_hbm, skin_hbm, out_ref,
    pot, typ, sat, pat, inv, cpl, skin, place, table, wbuf, gbuf, send, recv, bsend, brecv, csend, crecv, hsend, hrecv, rbuf, crbuf,
    load_sem, ready, wready, hready, allhere, ps, pr, cs, cr, bs, br, ws, wr, hs, hr, bds, bdr, fs, cfs,
):
    dom, x = lax.axis_index("dom"), lax.axis_index("cell")
    c, z, y = lax.rem(dom, 2), lax.rem(dom // 2, NZ), dom // (2 * NZ)

    def at(yy, zz, cc):
        return ((yy * NZ + zz) * 2 + cc, x)

    ahead = {d: lax.rem(z + d, NZ) for d in OFFSETS}
    behind = {d: lax.rem(z + NZ - d, NZ) for d in OFFSETS}
    zpeer = {d: at(y, ahead[d], c) for d in OFFSETS}
    special = jnp.logical_and(x == 0, jnp.logical_and(y == 0, c == 0))
    shift = special.astype(jnp.int32)

    def turn_of(zz):
        return jnp.where(jnp.logical_and(special, zz == 0), NZ, jnp.minimum(zz, HALF))

    def slot_of(zz):
        return jnp.where(zz < HALF, lax.rem(zz + HALF - shift, HALF), zz)

    zback = {d: at(y, behind[d], c) for d in OFFSETS}
    mine, slot = turn_of(z), slot_of(z)
    ahead_later = {d: turn_of(ahead[d]) > mine for d in OFFSETS}
    ahead_alike = {d: turn_of(ahead[d]) == mine for d in OFFSETS}
    ahead_earlier = {d: turn_of(ahead[d]) < mine for d in OFFSETS}
    ahead_last = {d: turn_of(ahead[d]) == NZ for d in OFFSETS}
    behind_earlier = {d: turn_of(behind[d]) < mine for d in OFFSETS}
    n_behind = jnp.where(mine == NZ, NZ - 1, mine - shift)
    early, late = mine < HALF, mine == HALF
    wpeer, later = {}, {}
    for k in range(1, 4):
        yy = lax.rem(y + NY - k, NY)
        wpeer[k] = at(yy, z, c)
        later[k] = yy > y
    wpeer[4] = at(y, z, 1 - c)
    later[4] = c == 1
    index = dom * NX + x
    after = ((index + 1) // NX, lax.rem(index + 1, NX))
    before = ((index - 1 + NX) // NX - 1, lax.rem(index - 1 + NX, NX))
    has_after, has_before = index < 2 * NY * NZ * NX - 1, index > 0

    ahead_next = jnp.logical_or(x < NX - 1, jnp.logical_and(c == 1, z < NZ - 1))
    behind_next = jnp.logical_or(x > 0, jnp.logical_and(c == 0, z > 0))
    i_first = jnp.logical_and(has_after, ahead_next)
    i_last = jnp.logical_and(has_after, jnp.logical_not(ahead_next))
    b_first = jnp.logical_and(has_before, behind_next)
    b_last = jnp.logical_and(has_before, jnp.logical_not(behind_next))
    relayed = mine < GROUP
    relays = jnp.logical_and(jnp.logical_and(z >= GROUP, z < 2 * GROUP), turn_of(z - GROUP) < GROUP)

    barrier = pltpu.get_barrier_semaphore()
    for d in OFFSETS:
        @pl.when(ahead_later[d])
        def _(d=d):
            pl.semaphore_signal(barrier, inc=1, device_id=zpeer[d], device_id_type=MESH)
    for k in wpeer:
        @pl.when(later[k])
        def _(k=k):
            pl.semaphore_signal(barrier, inc=1, device_id=wpeer[k], device_id_type=MESH)

    @pl.when(i_first)
    def _():
        pl.semaphore_signal(barrier, inc=1, device_id=after, device_id_type=MESH)

    @pl.when(b_last)
    def _():
        pl.semaphore_signal(barrier, inc=1, device_id=before, device_id_type=MESH)

    loads = [
        pltpu.make_async_copy(src, dst, load_sem.at[i])
        for i, (src, dst) in enumerate([
            (types_hbm, typ), (sat_hbm, sat), (pat_hbm, pat), (pot_hbm, pot), (inv_hbm, inv), (cpl_hbm, cpl),
            (skin_hbm, skin),
        ])
    ]
    for load in loads:
        load.start()
    n_earlier = y + 1 - c + n_behind + b_first.astype(jnp.int32) + i_last.astype(jnp.int32)

    @pl.when(n_earlier > 0)
    def _():
        pl.semaphore_wait(barrier, n_earlier)

    for d in reversed(OFFSETS):
        @pl.when(behind_earlier[d])
        def _(d=d):
            pl.semaphore_signal(ready.at[d], inc=1, device_id=zback[d], device_id_type=MESH)
    for k in wpeer:
        @pl.when(jnp.logical_not(later[k]))
        def _(k=k):
            at_peer = k if k == 4 else 4 - k
            pl.semaphore_signal(wready.at[at_peer], inc=1, device_id=wpeer[k], device_id_type=MESH)

    @pl.when(i_last)
    def _():
        pl.semaphore_signal(hready.at[1], inc=1, device_id=after, device_id_type=MESH)

    @pl.when(b_first)
    def _():
        pl.semaphore_signal(hready.at[0], inc=1, device_id=before, device_id_type=MESH)

    loads[4].wait()
    loads[5].wait()
    w = inv[...]
    wbuf[0, 0:128, :] = jnp.concatenate([w[0:128].astype(F32), w[128:256].astype(F32)], axis=1).astype(BF16)
    block = cpl[...].astype(F32)
    wbuf[0, 128:192, :] = jnp.concatenate([block, block.T], axis=1).astype(BF16)
    weights = {
        k: pltpu.make_async_remote_copy(
            wbuf.at[max(k - 4, 0)], wbuf.at[k], ws.at[k], wr.at[k], device_id=wpeer[min(k, 4)], device_id_type=MESH
        )
        for k in range(1, 8)
    }
    for want in (False, True):
        for k in (2, 1, 3, 4):
            if want and k == 4:
                continue

            @pl.when(later[k] == want)
            def _(k=k, want=want):
                if want:
                    pl.semaphore_wait(wready.at[k], 1)
                weights[k].start()

    for i in (0, 1, 2, 3, 6):
        loads[i].wait()

    field = pot[...]
    t = typ[...]
    onehot = (iota((128, 256), 0) == t).astype(BF16)
    earlier = (iota((256, 256), 0) < iota((256, 256), 1)).astype(BF16)
    rank = jnp.sum(onehot.astype(F32) * mm(onehot, earlier), axis=0, keepdims=True).astype(jnp.int32)
    t_y, t_z, t_c = t // (2 * NZ), (t // 2) % NZ, t % 2
    row = t_z * 16 + ((t_y - y + NY) % NY) * 4 + rank
    side = (t_c - c + 2) % 2
    both = jnp.concatenate([jnp.where(side == 0, row, -1), jnp.where(side == 1, row, -1)], axis=1)
    place[...] = (iota((256, 512), 0) == both).astype(BF16)
    level, bits = sat[...], pat[...]
    code = (1 + (level % 2) * 128 + bits) * jnp.where(level >= 2, -1, 1)
    code = jnp.broadcast_to(code.astype(F32), (64, 256)).astype(BF16)
    drive = field.astype(BF16)
    none = jnp.zeros((64, 256), BF16)
    spread = jnp.concatenate(
        [jnp.concatenate([a, none], axis=1) if i == 0 else jnp.concatenate([none, a], axis=1)
         for a in (drive, code) for i in range(2)], axis=0
    )
    placed = mm(place[...], spread, NT)
    keep = iota((NZ, 16, 128), 2) % 64 == iota((NZ, 16, 128), 1)
    send[...] = placed[:, 0:128].astype(BF16).reshape(NZ, 16, 128)
    csend[...] = jnp.sum(jnp.where(keep, placed[:, 128:256].reshape(NZ, 16, 128), 0.0), axis=1, keepdims=True)

    out, back, backin = {}, {}, {}
    for d in OFFSETS:
        out[d] = [
            pltpu.make_async_remote_copy(
                csend.at[ahead[d]], crecv.at[slot], cs.at[d], cr.at[d], device_id=zpeer[d], device_id_type=MESH
            ),
            pltpu.make_async_remote_copy(
                send.at[ahead[d]], recv.at[slot], ps.at[d], pr.at[d], device_id=zpeer[d], device_id_type=MESH
            ),
        ]
        back[d] = pltpu.make_async_remote_copy(
            bsend.at[slot_of(behind[d])], brecv.at[z], bs.at[d], br.at[d], device_id=zback[d], device_id_type=MESH
        )
    for d in OFFSETS:
        @pl.when(ahead_earlier[d])
        def _(d=d):
            for copy in out[d]:
                copy.start()

    eye = iota((64, 128), 0) == iota((64, 128), 1)
    hsend[0] = jnp.sum(jnp.where(eye, field[:, 255:256], 0.0), axis=0, keepdims=True)
    hsend[1] = jnp.sum(jnp.where(eye, field[:, 0:1], 0.0), axis=0, keepdims=True)
    to_after = pltpu.make_async_remote_copy(
        hsend.at[0], hrecv.at[0], hs.at[0], hr.at[0], device_id=after, device_id_type=MESH
    )
    to_before = pltpu.make_async_remote_copy(
        hsend.at[1], hrecv.at[1], hs.at[1], hr.at[1], device_id=before, device_id_type=MESH
    )

    pl.when(i_last)(to_after.start)
    pl.when(b_first)(to_before.start)

    span = pl.ds(lax.rem(z + FAR[0], NZ - len(FAR) + 1), len(FAR))
    bundle = [
        pltpu.make_async_remote_copy(
            src.at[span], dst, bds.at[i], bdr.at[i], device_id=zpeer[GROUP], device_id_type=MESH
        )
        for i, (src, dst) in enumerate([(csend, crbuf), (send, rbuf)])
    ]
    from_slot = slot_of(jnp.maximum(z - GROUP, 0))
    onward = {}
    for j in range(1, len(FAR) + 1):
        onward[j] = [
            pltpu.make_async_remote_copy(
                src.at[j - 1], dst.at[from_slot], ss.at[j - 1], rs.at[j + GROUP],
                device_id=zpeer[j], device_id_type=MESH,
            )
            for src, dst, ss, rs in ((crbuf, crecv, cfs, cr), (rbuf, recv, fs, pr))
        ]

    def send_on(d):
        goes = jnp.logical_and(jnp.logical_and(early, ahead_later[d]), jnp.logical_not(ahead_last[d]))

        @pl.when(jnp.logical_and(goes, jnp.logical_not(relayed)) if d in FAR else goes)
        def _():
            pl.semaphore_wait(ready.at[d], 1)
            for copy in out[d]:
                copy.start()

    for d in (*range(1, GROUP + 2), *range(NZ - 1, FAR[-1], -1), *range(FAR[-1], GROUP + 1, -1)):
        send_on(d)
        if d == GROUP:
            @pl.when(relayed)
            def _():
                for copy in bundle:
                    copy.start()

        if d in onward:
            @pl.when(relays)
            def _(d=d):
                if d == 1:
                    for copy in bundle:
                        copy.wait_recv()
                for copy in onward[d]:
                    copy.start()

    @pl.when(z == HALF - 1)
    def _():
        for d in range(1, GROUP + 1):
            pl.semaphore_signal(allhere, inc=1, device_id=zpeer[d], device_id_type=MESH)

    @pl.when(z == 1)
    def _():
        for d in range(HALF - 1, FAR[-1] + 1):
            pl.semaphore_wait(ready.at[d], 1)
        for d in range(NZ - 2, NZ - 2 - GROUP, -1):
            pl.semaphore_signal(allhere, inc=1, device_id=zpeer[d], device_id_type=MESH)

    @pl.when(later[4])
    def _():
        pl.semaphore_wait(wready.at[4], 1)
        weights[4].start()

    recv[slot] = send[z]
    crecv[slot] = csend[z]

    @pl.when(i_first)
    def _():
        pl.semaphore_wait(hready.at[0], 1)
        to_after.start()

    table[...] = coefficients(skin)
    total = skin[0]
    for k in range(1, 8):
        total = total + skin[k]

    gbuf[0] = product(wbuf[0, 0:128, :], wbuf[0, 128:192, :])
    for k in (1, 3, 2):
        weights[k].wait_recv()
        weights[k + 4].start()
    for k in (1, 3, 2, 4, 5, 7, 6):
        if k >= 4:
            weights[k].wait_recv()
        gbuf[k] = product(wbuf[k, 0:128, :], wbuf[k, 128:192, :])

    spreads = table[...]
    for start, stop in ((0, GROUP), (GROUP, 2 * GROUP), (2 * GROUP, NZ)):
        for d in OFFSETS:
            @pl.when(jnp.logical_and(slot_of(behind[d]) >= start, slot_of(behind[d]) < stop))
            def _(d=d):
                for copy in out[d]:
                    copy.wait_recv()
        n = stop - start
        answer = solve(
            recv[start:stop].reshape(n * 16, 128), crecv[start:stop].reshape(n, 128), wbuf, gbuf, spreads, total
        )
        bsend[start:stop] = answer.reshape(n, 16, 128)
        for d in reversed(OFFSETS):
            @pl.when(jnp.logical_and(slot_of(behind[d]) >= start, slot_of(behind[d]) < stop))
            def _(d=d):
                back[d].start()
        if start == 0:
            @pl.when(late)
            def _():
                pl.semaphore_wait(allhere, 1)
                for d in OFFSETS:
                    @pl.when(ahead_alike[d])
                    def _(d=d):
                        for copy in out[d]:
                            copy.start()

            for d in OFFSETS:
                @pl.when(ahead_last[d])
                def _(d=d):
                    pl.semaphore_wait(ready.at[d], 1)
                    for copy in out[d]:
                        copy.start()
    brecv[z] = bsend[slot]

    @pl.when(b_last)
    def _():
        pl.semaphore_wait(hready.at[1], 1)
        to_before.start()

    pl.when(has_before)(to_after.wait_recv)
    pl.when(has_after)(to_before.wait_recv)
    lane = iota((64, 256), 1)
    left = jnp.sum(jnp.where(jnp.logical_and(eye, has_before), hrecv[0], 0.0), axis=1, keepdims=True)
    right = jnp.sum(jnp.where(jnp.logical_and(eye, has_after), hrecv[1], 0.0), axis=1, keepdims=True)
    left = jnp.where(lane == 0, left, pltpu.roll(field, 1, 1))
    right = jnp.where(lane == 255, right, pltpu.roll(field, 255, 1))
    pot[...] = field + 0.25 * (left - 2.0 * field + right)

    for d in OFFSETS:
        back[d].wait_recv()
    got = mm(brecv[...].reshape(256, 128), place[...], TN)
    out_ref[...] = pot[...] - (got[0:64, 0:256] + got[64:128, 256:512])

    for k in weights:
        weights[k].wait_send()
    for d in OFFSETS:
        if d in FAR:
            @pl.when(jnp.logical_not(relayed))
            def _(d=d):
                for copy in out[d]:
                    copy.wait_send()

            @pl.when(jnp.logical_and(relayed, z != 1) if d >= HALF - 1 else relayed)
            def _(d=d):
                pl.semaphore_wait(ready.at[d], 1)
        else:
            for copy in out[d]:
                copy.wait_send()
        back[d].wait_send()

    @pl.when(relayed)
    def _():
        for copy in bundle:
            copy.wait_send()

    @pl.when(relays)
    def _():
        for j in onward:
            for copy in onward[j]:
                copy.wait_send()

    pl.when(has_after)(to_after.wait_send)
    pl.when(has_before)(to_before.wait_send)


def body(potential, types, saturation, pattern, inverses, coupling, skin):
    dma = pltpu.SemaphoreType.DMA
    return pl.pallas_call(
        kernel,
        out_shape=jax.ShapeDtypeStruct((64, 256), F32),
        in_specs=[pl.BlockSpec(memory_space=pl.ANY)] * 7,
        out_specs=pl.BlockSpec(memory_space=pltpu.VMEM),
        scratch_shapes=[
            pltpu.VMEM((64, 256), F32),
            pltpu.VMEM((1, 256), jnp.int32),
            pltpu.VMEM((1, 256), jnp.int32),
            pltpu.VMEM((1, 256), jnp.int32),
            pltpu.VMEM((256, 64), BF16),
            pltpu.VMEM((64, 64), BF16),
            pltpu.SMEM((8,), F32),
            pltpu.VMEM((256, 512), BF16),
            pltpu.VMEM((128, 768), BF16),
            pltpu.VMEM((8, 192, 128), BF16),
            pltpu.VMEM((8, 256, 128), BF16),
            pltpu.VMEM((NZ, 16, 128), BF16),
            pltpu.VMEM((NZ, 16, 128), BF16),
            pltpu.VMEM((NZ, 16, 128), BF16),
            pltpu.VMEM((NZ, 16, 128), BF16),
            pltpu.VMEM((NZ, 1, 128), F32),
            pltpu.VMEM((NZ, 1, 128), F32),
            pltpu.VMEM((2, 1, 128), F32),
            pltpu.VMEM((2, 1, 128), F32),
            pltpu.VMEM((len(FAR), 16, 128), BF16),
            pltpu.VMEM((len(FAR), 1, 128), F32),
            dma((7,)),
            pltpu.SemaphoreType.REGULAR((NZ,)),
            pltpu.SemaphoreType.REGULAR((8,)),
            pltpu.SemaphoreType.REGULAR((2,)),
            pltpu.SemaphoreType.REGULAR,
            *[dma((NZ,)) for _ in range(6)],
            *[dma((8,)) for _ in range(2)],
            *[dma((2,)) for _ in range(4)],
            *[dma((len(FAR),)) for _ in range(2)],
        ],
        compiler_params=pltpu.CompilerParams(
            collective_id=0, has_side_effects=True, vmem_limit_bytes=64 * 1024 * 1024
        ),
        name="regroup_solve",
    )(
        potential,
        types.reshape(1, 256),
        saturation.reshape(1, 256),
        pattern.reshape(1, 256),
        inverses.reshape(256, 64),
        coupling.reshape(64, 64),
        skin,
    )


def solution(mesh):
    placed = (
        P(None, ("dom", "cell")),
        P(("dom", "cell"), None),
        P(("dom", "cell")),
        P(("dom", "cell")),
        P("dom", None, None, None),
        P("dom", None, None),
        P(),
    )
    return jax.shard_map(
        body, mesh=mesh, in_specs=placed, out_specs=P(None, ("dom", "cell")), check_vma=False
    )
```

time: 35.1 us -> 35.2 us (level)
  the two profiles are of different devices: /device:TPU:32 before, /device:TPU:24 now
where the time goes in v4:
time: 35.2 us; the launch traced here: 34.5 us
  Pallas kernels  33.1 us (94%)
  local copies, waits for them, and re-layouts  1.47 us (4%)
    pallas_call x1, Pallas kernels, body(): pl.pallas_call(kernel, out_shape=jax.ShapeDtypeStruct((64, 256), F32), in...  33.1 us
    unnamed x1, local copies, waits for them, and re-layouts  1.47 us

profile of v4, /device:TPU:24, one launch (start us, length us, event | category | flops | bytes accessed | tf_op | source)
XLA Modules:
  0.0 34.5 jit_solution(9062991704438694841)
XLA Ops:
  0.0 33.1 %regroup_solve.1 = f32[64,256]{1,0:T(8,128)} custom-call(f32[64,256]{1,0:T(8,128)} %pot_hbm.1, s32[1,256]{1,0:T(1,128)} %bitcast.7, s32[1,256]{1,0:T(1,128)} %bitcast.8, s32[1,256]{1,0:T(1,128)} %bitcast.9, bf16[256,64]{1,0:T(8,128)(2,1)} %bitcast.5, bf16[64,64]{1,0:T(8,128)(2,1)} %bitcast.6, f32[8]{0:T(128)} %skin_hbm.1), custom_call_target="tpu_custom_call" | custom-call | tf_op jit(solution)/shard_map/regroup_solve/pallas_call | solution.py:475
  33.1 1.5 %copy.9 = f32[64,256]{1,0:T(8,128)} copy(f32[64,256]{1,0:T(8,128)} %regroup_solve.1) | data formatting | bytes 131072

commit v5 on v4

--- a/solution.py
+++ b/solution.py
@@ -137,17 +137,26 @@
         return jnp.where(jnp.logical_and(special, zz == 0), NZ, jnp.minimum(zz, HALF))
 
     def slot_of(zz):
-        return jnp.where(zz < HALF, lax.rem(zz + HALF - shift, HALF), zz)
+        return jnp.where(jnp.logical_and(special, zz == 0), HALF, zz + (zz >= HALF).astype(jnp.int32))
 
     zback = {d: at(y, behind[d], c) for d in OFFSETS}
     mine, slot = turn_of(z), slot_of(z)
-    ahead_later = {d: turn_of(ahead[d]) > mine for d in OFFSETS}
-    ahead_alike = {d: turn_of(ahead[d]) == mine for d in OFFSETS}
-    ahead_earlier = {d: turn_of(ahead[d]) < mine for d in OFFSETS}
-    ahead_last = {d: turn_of(ahead[d]) == NZ for d in OFFSETS}
-    behind_earlier = {d: turn_of(behind[d]) < mine for d in OFFSETS}
-    n_behind = jnp.where(mine == NZ, NZ - 1, mine - shift)
-    early, late = mine < HALF, mine == HALF
+    def apart(a, b):
+        far = jnp.logical_and(b >= HALF, b < HALF + GROUP)
+        return jnp.logical_and(special, jnp.logical_and(a == 0, far))
+
+    def alike(zz):
+        return jnp.logical_or(turn_of(zz) == mine, jnp.logical_or(apart(z, zz), apart(zz, z)))
+
+    ahead_alike = {d: alike(ahead[d]) for d in OFFSETS}
+    ahead_later = {d: jnp.logical_and(turn_of(ahead[d]) > mine, jnp.logical_not(ahead_alike[d])) for d in OFFSETS}
+    ahead_earlier = {d: jnp.logical_and(turn_of(ahead[d]) < mine, jnp.logical_not(ahead_alike[d])) for d in OFFSETS}
+    ahead_last = {d: jnp.logical_and(turn_of(ahead[d]) == NZ, jnp.logical_not(ahead_alike[d])) for d in OFFSETS}
+    behind_earlier = {
+        d: jnp.logical_and(turn_of(behind[d]) < mine, jnp.logical_not(alike(behind[d]))) for d in OFFSETS
+    }
+    n_behind = jnp.where(mine == NZ, NZ - 1 - GROUP, mine - shift)
+    early, late, lone = mine < HALF, mine == HALF, mine == NZ
     wpeer, later = {}, {}
     for k in range(1, 4):
         yy = lax.rem(y + NY - k, NY)
@@ -346,23 +355,47 @@
                 for copy in onward[d]:
                     copy.start()
 
-    @pl.when(z == HALF - 1)
-    def _():
-        for d in range(1, GROUP + 1):
-            pl.semaphore_signal(allhere, inc=1, device_id=zpeer[d], device_id_type=MESH)
-
-    @pl.when(z == 1)
-    def _():
-        for d in range(HALF - 1, FAR[-1] + 1):
-            pl.semaphore_wait(ready.at[d], 1)
-        for d in range(NZ - 2, NZ - 2 - GROUP, -1):
-            pl.semaphore_signal(allhere, inc=1, device_id=zpeer[d], device_id_type=MESH)
+    def tell(when, at_offset, told):
+        @pl.when(when)
+        def _():
+            @pl.when(special)
+            def _():
+                pl.semaphore_wait(ready.at[at_offset], 1)
+                for copy in out[at_offset]:
+                    copy.start()
+
+            if told[0] != 1:
+                for d in range(HALF - 1, FAR[-1] + 1):
+                    pl.semaphore_wait(ready.at[d], 1)
+
+                @pl.when(special)
+                def _():
+                    pl.semaphore_signal(allhere, inc=1, device_id=zpeer[at_offset], device_id_type=MESH)
+
+            for d in told:
+                pl.semaphore_signal(allhere, inc=1, device_id=zpeer[d], device_id_type=MESH)
+
+    tell(z == HALF - 1, HALF + 1, range(1, GROUP + 1))
+    tell(z == 1, NZ - 1, range(NZ - 2, NZ - 2 - GROUP, -1))
+
+    def send_alike():
+        pl.semaphore_wait(allhere, 1)
+        for d in OFFSETS:
+            @pl.when(ahead_alike[d])
+            def _(d=d):
+                for copy in out[d]:
+                    copy.start()
+
+    pl.when(lone)(send_alike)
 
     @pl.when(later[4])
     def _():
         pl.semaphore_wait(wready.at[4], 1)
         weights[4].start()
 
+    empty = jnp.where(special, 0, HALF)
+    recv[empty] = jnp.zeros((16, 128), BF16)
+    crecv[empty] = jnp.zeros((1, 128), F32)
     recv[slot] = send[z]
     crecv[slot] = csend[z]
 
@@ -370,6 +403,11 @@
     def _():
         pl.semaphore_wait(hready.at[0], 1)
         to_after.start()
+
+    @pl.when(jnp.logical_and(b_last, z > 0))
+    def _():
+        pl.semaphore_wait(hready.at[1], 1)
+        to_before.start()
 
     table[...] = coefficients(skin)
     total = skin[0]
@@ -386,7 +424,7 @@
         gbuf[k] = product(wbuf[k, 0:128, :], wbuf[k, 128:192, :])
 
     spreads = table[...]
-    for start, stop in ((0, GROUP), (GROUP, 2 * GROUP), (2 * GROUP, NZ)):
+    for start, stop in ((0, GROUP), (GROUP, HALF + 1), (HALF + 1, NZ + 1)):
         for d in OFFSETS:
             @pl.when(jnp.logical_and(slot_of(behind[d]) >= start, slot_of(behind[d]) < stop))
             def _(d=d):
@@ -402,24 +440,16 @@
             def _(d=d):
                 back[d].start()
         if start == 0:
-            @pl.when(late)
-            def _():
-                pl.semaphore_wait(allhere, 1)
-                for d in OFFSETS:
-                    @pl.when(ahead_alike[d])
-                    def _(d=d):
-                        for copy in out[d]:
-                            copy.start()
-
+            pl.when(late)(send_alike)
             for d in OFFSETS:
-                @pl.when(ahead_last[d])
+                @pl.when(jnp.logical_and(ahead_last[d], jnp.logical_and(z != 1, z != HALF - 1)))
                 def _(d=d):
                     pl.semaphore_wait(ready.at[d], 1)
                     for copy in out[d]:
                         copy.start()
     brecv[z] = bsend[slot]
 
-    @pl.when(b_last)
+    @pl.when(jnp.logical_and(b_last, z == 0))
     def _():
         pl.semaphore_wait(hready.at[1], 1)
         to_before.start()
@@ -490,11 +520,11 @@
             pltpu.VMEM((8, 192, 128), BF16),
             pltpu.VMEM((8, 256, 128), BF16),
             pltpu.VMEM((NZ, 16, 128), BF16),
-            pltpu.VMEM((NZ, 16, 128), BF16),
-            pltpu.VMEM((NZ, 16, 128), BF16),
+            pltpu.VMEM((NZ + 1, 16, 128), BF16),
+            pltpu.VMEM((NZ + 1, 16, 128), BF16),
             pltpu.VMEM((NZ, 16, 128), BF16),
             pltpu.VMEM((NZ, 1, 128), F32),
-            pltpu.VMEM((NZ, 1, 128), F32),
+            pltpu.VMEM((NZ + 1, 1, 128), F32),
             pltpu.VMEM((2, 1, 128), F32),
             pltpu.VMEM((2, 1, 128), F32),
             pltpu.VMEM((len(FAR), 16, 128), BF16),
@@ -510,17 +540,22 @@
             *[dma((len(FAR),)) for _ in range(2)],
         ],
         compiler_params=pltpu.CompilerParams(
-            collective_id=0, has_side_effects=True, vmem_limit_bytes=64 * 1024 * 1024
+            collective_id=0, has_side_effects=True, vmem_limit_bytes=32 * 1024 * 1024
         ),
         name="regroup_solve",
     )(
-        potential,
-        types.reshape(1, 256),
-        saturation.reshape(1, 256),
-        pattern.reshape(1, 256),
-        inverses.reshape(256, 64),
-        coupling.reshape(64, 64),
-        skin,
+        *[
+            pltpu.with_memory_space_constraint(array, pltpu.HBM)
+            for array in (
+                potential,
+                types.reshape(1, 256),
+                saturation.reshape(1, 256),
+                pattern.reshape(1, 256),
+                inverses.reshape(256, 64),
+                coupling.reshape(64, 64),
+                skin,
+            )
+        ]
     )
 
 

time: 35.2 us -> 33.5 us (0.952); the launches traced: 34.5 us -> 33.3 us
  local copies, waits for them, and re-layouts: 1.47 us -> 0.63 us
  Pallas kernels: 33.1 us -> 32.7 us
    unnamed x1, local copies, waits for them, and re-layouts: 1.47 us -> 0.63 us
    pallas_call x1, Pallas kernels: 33.1 us -> 32.7 us  [body(): pl.pallas_call(kernel, out_shape=jax.ShapeDtypeStruct((64, 256), F32), in...]
where the time goes in v5:
time: 33.5 us; the launch traced here: 33.3 us
  Pallas kernels  32.7 us (98%)
  local copies, waits for them, and re-layouts  0.63 us (2%)
    pallas_call x1, Pallas kernels, body(): pl.pallas_call(kernel, out_shape=jax.ShapeDtypeStruct((64, 256), F32), in...  32.7 us

profile of v5, /device:TPU:24, one launch (start us, length us, event | category | flops | bytes accessed | tf_op | source)
XLA Modules:
  0.0 33.3 jit_solution(7517183278114039569)
XLA Ops:
  0.0 32.7 %regroup_solve.1 = f32[64,256]{1,0:T(8,128)S(1)} custom-call(f32[64,256]{1,0:T(8,128)} %pot_hbm.1, s32[1,256]{1,0:T(1,128)} %bitcast.7, s32[1,256]{1,0:T(1,128)} %bitcast.8, s32[1,256]{1,0:T(1,128)} %bitcast.9, bf16[256,64]{1,0:T(8,128)(2,1)} %bitcast.5, bf16[64,64]{1,0:T(8,128)(2,1)} %bitcast.6, f32[8]{0:T(128)} %skin_hbm.1), custom_call_target="tpu_custom_call" | custom-call | tf_op jit(solution)/shard_map/regroup_solve/pallas_call | solution.py:505
  32.7 0.6 %copy.9 = f32[64,256]{1,0:T(8,128)} copy(f32[64,256]{1,0:T(8,128)S(1)} %regroup_solve.1) | data formatting | bytes 131072

commit v6 on v5

--- a/solution.py
+++ b/solution.py
@@ -119,7 +119,7 @@
 def kernel(
     pot_hbm, types_hbm, sat_hbm, pat_hbm, inv_hbm, cpl_hbm, skin_hbm, out_ref,
     pot, typ, sat, pat, inv, cpl, skin, place, table, wbuf, gbuf, send, recv, bsend, brecv, csend, crecv, hsend, hrecv, rbuf, crbuf,
-    load_sem, ready, wready, hready, allhere, ps, pr, cs, cr, bs, br, ws, wr, hs, hr, bds, bdr, fs, cfs,
+    load_sem, ready, wready, hready, allhere, rowhere, ps, pr, cs, cr, bs, br, ws, wr, hs, hr, bds, bdr, fs, cfs,
 ):
     dom, x = lax.axis_index("dom"), lax.axis_index("cell")
     c, z, y = lax.rem(dom, 2), lax.rem(dom // 2, NZ), dom // (2 * NZ)
@@ -137,7 +137,7 @@
         return jnp.where(jnp.logical_and(special, zz == 0), NZ, jnp.minimum(zz, HALF))
 
     def slot_of(zz):
-        return jnp.where(jnp.logical_and(special, zz == 0), HALF, zz + (zz >= HALF).astype(jnp.int32))
+        return jnp.where(jnp.logical_and(special, zz == 0), HALF, zz + (zz >= HALF) * 1)
 
     zback = {d: at(y, behind[d], c) for d in OFFSETS}
     mine, slot = turn_of(z), slot_of(z)
@@ -171,9 +171,13 @@
 
     ahead_next = jnp.logical_or(x < NX - 1, jnp.logical_and(c == 1, z < NZ - 1))
     behind_next = jnp.logical_or(x > 0, jnp.logical_and(c == 0, z > 0))
-    i_first = jnp.logical_and(has_after, ahead_next)
+    part_after = jnp.logical_and(jnp.logical_and(x == NX - 1, c == 1), jnp.logical_and(z > 0, z < NZ - 1))
+    part_before = jnp.logical_and(jnp.logical_and(x == 0, c == 0), z > 1)
+    tells_after = jnp.logical_and(jnp.logical_and(x == NX - 1, c == 1), z == 0)
+    tells_before = jnp.logical_and(jnp.logical_and(x == 0, c == 0), z == 1)
+    i_first = jnp.logical_and(has_after, jnp.logical_and(ahead_next, jnp.logical_not(part_after)))
     i_last = jnp.logical_and(has_after, jnp.logical_not(ahead_next))
-    b_first = jnp.logical_and(has_before, behind_next)
+    b_first = jnp.logical_and(has_before, jnp.logical_and(behind_next, jnp.logical_not(part_before)))
     b_last = jnp.logical_and(has_before, jnp.logical_not(behind_next))
     relayed = mine < GROUP
     relays = jnp.logical_and(jnp.logical_and(z >= GROUP, z < 2 * GROUP), turn_of(z - GROUP) < GROUP)
@@ -355,6 +359,11 @@
                 for copy in onward[d]:
                     copy.start()
 
+    @pl.when(relayed)
+    def _():
+        for d in FAR:
+            pl.semaphore_wait(ready.at[d], 1)
+
     def tell(when, at_offset, told):
         @pl.when(when)
         def _():
@@ -365,9 +374,6 @@
                     copy.start()
 
             if told[0] != 1:
-                for d in range(HALF - 1, FAR[-1] + 1):
-                    pl.semaphore_wait(ready.at[d], 1)
-
                 @pl.when(special)
                 def _():
                     pl.semaphore_signal(allhere, inc=1, device_id=zpeer[at_offset], device_id_type=MESH)
@@ -408,6 +414,14 @@
     def _():
         pl.semaphore_wait(hready.at[1], 1)
         to_before.start()
+
+    @pl.when(tells_after)
+    def _():
+        pl.semaphore_signal(rowhere, inc=1, device_id=after, device_id_type=MESH)
+
+    @pl.when(tells_before)
+    def _():
+        pl.semaphore_signal(rowhere, inc=1, device_id=before, device_id_type=MESH)
 
     table[...] = coefficients(skin)
     total = skin[0]
@@ -425,22 +439,39 @@
 
     spreads = table[...]
     for start, stop in ((0, GROUP), (GROUP, HALF + 1), (HALF + 1, NZ + 1)):
-        for d in OFFSETS:
-            @pl.when(jnp.logical_and(slot_of(behind[d]) >= start, slot_of(behind[d]) < stop))
-            def _(d=d):
-                for copy in out[d]:
-                    copy.wait_recv()
+        sources = [j for j in range(NZ) if start <= j + (j >= HALF) < stop] + ([0] if start == GROUP else [])
+        apply = {j: (special if start == GROUP else jnp.logical_not(special)) if j == 0 else True for j in sources}
+        for j in sources:
+            @pl.when(jnp.logical_and(z != j, apply[j]))
+            def _(j=j):
+                d = lax.rem(z - j + NZ, NZ)
+                for src, dst, ss, rs in ((csend, crecv, cs, cr), (send, recv, ps, pr)):
+                    pltpu.make_async_remote_copy(
+                        src.at[j], dst.at[j], ss.at[d], rs.at[d], device_id=at(y, j, c), device_id_type=MESH
+                    ).wait_recv()
+
         n = stop - start
         answer = solve(
             recv[start:stop].reshape(n * 16, 128), crecv[start:stop].reshape(n, 128), wbuf, gbuf, spreads, total
         )
         bsend[start:stop] = answer.reshape(n, 16, 128)
-        for d in reversed(OFFSETS):
-            @pl.when(jnp.logical_and(slot_of(behind[d]) >= start, slot_of(behind[d]) < stop))
-            def _(d=d):
-                back[d].start()
+        for j in sources:
+            @pl.when(jnp.logical_and(z != j, apply[j]))
+            def _(j=j):
+                d = lax.rem(z - j + NZ, NZ)
+                pltpu.make_async_remote_copy(
+                    bsend.at[slot_of(j)], brecv.at[z], bs.at[d], br.at[d], device_id=at(y, j, c), device_id_type=MESH
+                ).start()
+
         if start == 0:
             pl.when(late)(send_alike)
+
+            @pl.when(jnp.logical_or(tells_after, tells_before))
+            def _():
+                pl.semaphore_wait(rowhere, 1)
+                for d in range(1, NZ - 1):
+                    pl.semaphore_signal(rowhere, inc=1, device_id=zpeer[d], device_id_type=MESH)
+
             for d in OFFSETS:
                 @pl.when(jnp.logical_and(ahead_last[d], jnp.logical_and(z != 1, z != HALF - 1)))
                 def _(d=d):
@@ -452,6 +483,16 @@
     @pl.when(jnp.logical_and(b_last, z == 0))
     def _():
         pl.semaphore_wait(hready.at[1], 1)
+        to_before.start()
+
+    @pl.when(part_after)
+    def _():
+        pl.semaphore_wait(rowhere, 1)
+        to_after.start()
+
+    @pl.when(part_before)
+    def _():
+        pl.semaphore_wait(rowhere, 1)
         to_before.start()
 
     pl.when(has_before)(to_after.wait_recv)
@@ -463,11 +504,6 @@
     right = jnp.where(lane == 255, right, pltpu.roll(field, 255, 1))
     pot[...] = field + 0.25 * (left - 2.0 * field + right)
 
-    for d in OFFSETS:
-        back[d].wait_recv()
-    got = mm(brecv[...].reshape(256, 128), place[...], TN)
-    out_ref[...] = pot[...] - (got[0:64, 0:256] + got[64:128, 256:512])
-
     for k in weights:
         weights[k].wait_send()
     for d in OFFSETS:
@@ -476,10 +512,6 @@
             def _(d=d):
                 for copy in out[d]:
                     copy.wait_send()
-
-            @pl.when(jnp.logical_and(relayed, z != 1) if d >= HALF - 1 else relayed)
-            def _(d=d):
-                pl.semaphore_wait(ready.at[d], 1)
         else:
             for copy in out[d]:
                 copy.wait_send()
@@ -498,6 +530,11 @@
 
     pl.when(has_after)(to_after.wait_send)
     pl.when(has_before)(to_before.wait_send)
+
+    for d in OFFSETS:
+        back[d].wait_recv()
+    got = mm(brecv[...].reshape(256, 128), place[...], TN)
+    out_ref[...] = pot[...] - (got[0:64, 0:256] + got[64:128, 256:512])
 
 
 def body(potential, types, saturation, pattern, inverses, coupling, skin):
@@ -534,6 +571,7 @@
             pltpu.SemaphoreType.REGULAR((8,)),
             pltpu.SemaphoreType.REGULAR((2,)),
             pltpu.SemaphoreType.REGULAR,
+            pltpu.SemaphoreType.REGULAR,
             *[dma((NZ,)) for _ in range(6)],
             *[dma((8,)) for _ in range(2)],
             *[dma((2,)) for _ in range(4)],

time: 33.5 us -> 32 us (0.955)
  Pallas kernels: 32.7 us -> 31.2 us
    pallas_call x1, Pallas kernels: 32.7 us -> 31.2 us  [body(): pl.pallas_call(kernel, out_shape=jax.ShapeDtypeStruct((64, 256), F32), in...]
where the time goes in v6:
time: 32 us; the launch traced here: 31.8 us
  Pallas kernels  31.2 us (98%)
  local copies, waits for them, and re-layouts  0.63 us (2%)
    pallas_call x1, Pallas kernels, body(): pl.pallas_call(kernel, out_shape=jax.ShapeDtypeStruct((64, 256), F32), in...  31.2 us

profile of v6, /device:TPU:24, one launch (start us, length us, event | category | flops | bytes accessed | tf_op | source)
XLA Modules:
  0.0 31.8 jit_solution(1051033739729459297)
XLA Ops:
  0.0 31.2 %regroup_solve.1 = f32[64,256]{1,0:T(8,128)S(1)} custom-call(f32[64,256]{1,0:T(8,128)} %pot_hbm.1, s32[1,256]{1,0:T(1,128)} %bitcast.7, s32[1,256]{1,0:T(1,128)} %bitcast.8, s32[1,256]{1,0:T(1,128)} %bitcast.9, bf16[256,64]{1,0:T(8,128)(2,1)} %bitcast.5, bf16[64,64]{1,0:T(8,128)(2,1)} %bitcast.6, f32[8]{0:T(128)} %skin_hbm.1), custom_call_target="tpu_custom_call" | custom-call | tf_op jit(solution)/shard_map/regroup_solve/pallas_call | solution.py:542
  31.2 0.6 %copy.9 = f32[64,256]{1,0:T(8,128)} copy(f32[64,256]{1,0:T(8,128)S(1)} %regroup_solve.1) | data formatting | bytes 131072

commit v7 on v6

--- a/solution.py
+++ b/solution.py
@@ -122,13 +122,13 @@
     load_sem, ready, wready, hready, allhere, rowhere, ps, pr, cs, cr, bs, br, ws, wr, hs, hr, bds, bdr, fs, cfs,
 ):
     dom, x = lax.axis_index("dom"), lax.axis_index("cell")
-    c, z, y = lax.rem(dom, 2), lax.rem(dom // 2, NZ), dom // (2 * NZ)
+    c, z, y = dom & 1, (dom >> 1) & (NZ - 1), dom >> 5
 
     def at(yy, zz, cc):
         return ((yy * NZ + zz) * 2 + cc, x)
 
-    ahead = {d: lax.rem(z + d, NZ) for d in OFFSETS}
-    behind = {d: lax.rem(z + NZ - d, NZ) for d in OFFSETS}
+    ahead = {d: (z + d) & (NZ - 1) for d in OFFSETS}
+    behind = {d: (z - d) & (NZ - 1) for d in OFFSETS}
     zpeer = {d: at(y, ahead[d], c) for d in OFFSETS}
     special = jnp.logical_and(x == 0, jnp.logical_and(y == 0, c == 0))
     shift = special.astype(jnp.int32)
@@ -141,32 +141,19 @@
 
     zback = {d: at(y, behind[d], c) for d in OFFSETS}
     mine, slot = turn_of(z), slot_of(z)
-    def apart(a, b):
-        far = jnp.logical_and(b >= HALF, b < HALF + GROUP)
-        return jnp.logical_and(special, jnp.logical_and(a == 0, far))
-
-    def alike(zz):
-        return jnp.logical_or(turn_of(zz) == mine, jnp.logical_or(apart(z, zz), apart(zz, z)))
-
-    ahead_alike = {d: alike(ahead[d]) for d in OFFSETS}
-    ahead_later = {d: jnp.logical_and(turn_of(ahead[d]) > mine, jnp.logical_not(ahead_alike[d])) for d in OFFSETS}
-    ahead_earlier = {d: jnp.logical_and(turn_of(ahead[d]) < mine, jnp.logical_not(ahead_alike[d])) for d in OFFSETS}
-    ahead_last = {d: jnp.logical_and(turn_of(ahead[d]) == NZ, jnp.logical_not(ahead_alike[d])) for d in OFFSETS}
-    behind_earlier = {
-        d: jnp.logical_and(turn_of(behind[d]) < mine, jnp.logical_not(alike(behind[d]))) for d in OFFSETS
-    }
     n_behind = jnp.where(mine == NZ, NZ - 1 - GROUP, mine - shift)
+    middle = jnp.logical_and(z >= HALF, z < HALF + GROUP)
     early, late, lone = mine < HALF, mine == HALF, mine == NZ
     wpeer, later = {}, {}
     for k in range(1, 4):
-        yy = lax.rem(y + NY - k, NY)
+        yy = (y - k) & (NY - 1)
         wpeer[k] = at(yy, z, c)
         later[k] = yy > y
     wpeer[4] = at(y, z, 1 - c)
     later[4] = c == 1
     index = dom * NX + x
-    after = ((index + 1) // NX, lax.rem(index + 1, NX))
-    before = ((index - 1 + NX) // NX - 1, lax.rem(index - 1 + NX, NX))
+    after = ((index + 1) >> 2, (index + 1) & (NX - 1))
+    before = ((index - 1) >> 2, (index - 1) & (NX - 1))
     has_after, has_before = index < 2 * NY * NZ * NX - 1, index > 0
 
     ahead_next = jnp.logical_or(x < NX - 1, jnp.logical_and(c == 1, z < NZ - 1))
@@ -183,11 +170,18 @@
     relays = jnp.logical_and(jnp.logical_and(z >= GROUP, z < 2 * GROUP), turn_of(z - GROUP) < GROUP)
 
     barrier = pltpu.get_barrier_semaphore()
-    for d in OFFSETS:
-        @pl.when(ahead_later[d])
-        def _(d=d):
-            pl.semaphore_signal(barrier, inc=1, device_id=zpeer[d], device_id_type=MESH)
-    for k in wpeer:
+    @pl.when(early)
+    def _():
+        for j in range(1, NZ):
+            @pl.when(z < j)
+            def _(j=j):
+                pl.semaphore_signal(barrier, inc=1, device_id=at(y, j, c), device_id_type=MESH)
+
+    @pl.when(jnp.logical_and(jnp.logical_and(special, z > 0), jnp.logical_not(middle)))
+    def _():
+        pl.semaphore_signal(barrier, inc=1, device_id=at(y, 0, c), device_id_type=MESH)
+
+    for k in (1, 3, 4):
         @pl.when(later[k])
         def _(k=k):
             pl.semaphore_signal(barrier, inc=1, device_id=wpeer[k], device_id_type=MESH)
@@ -209,17 +203,25 @@
     ]
     for load in loads:
         load.start()
-    n_earlier = y + 1 - c + n_behind + b_first.astype(jnp.int32) + i_last.astype(jnp.int32)
+    n_earlier = jnp.minimum(y, 1) + y // 3 + 1 - c + n_behind + b_first.astype(jnp.int32) + i_last.astype(jnp.int32)
 
     @pl.when(n_earlier > 0)
     def _():
         pl.semaphore_wait(barrier, n_earlier)
 
-    for d in reversed(OFFSETS):
-        @pl.when(behind_earlier[d])
-        def _(d=d):
-            pl.semaphore_signal(ready.at[d], inc=1, device_id=zback[d], device_id_type=MESH)
-    for k in wpeer:
+    near_lone = (*range(1, HALF), *range(HALF + GROUP, NZ))
+    precedes = {j: jnp.logical_and(z > 0, jnp.logical_not(special)) if j == 0 else z > j for j in range(HALF)}
+    for j in range(HALF):
+        @pl.when(precedes[j])
+        def _(j=j):
+            pl.semaphore_signal(ready.at[(z - j) & (NZ - 1)], inc=1, device_id=at(y, j, c), device_id_type=MESH)
+
+    @pl.when(lone)
+    def _():
+        for j in near_lone:
+            pl.semaphore_signal(ready.at[NZ - j], inc=1, device_id=at(y, j, c), device_id_type=MESH)
+
+    for k in (1, 3, 4):
         @pl.when(jnp.logical_not(later[k]))
         def _(k=k):
             at_peer = k if k == 4 else 4 - k
@@ -246,7 +248,7 @@
         for k in range(1, 8)
     }
     for want in (False, True):
-        for k in (2, 1, 3, 4):
+        for k in (3, 1, 4):
             if want and k == 4:
                 continue
 
@@ -255,6 +257,11 @@
                 if want:
                     pl.semaphore_wait(wready.at[k], 1)
                 weights[k].start()
+
+    @pl.when(jnp.logical_and(y > 0, later[3]))
+    def _():
+        for k in (3, 1):
+            pl.semaphore_signal(wready.at[2], inc=1, device_id=wpeer[k], device_id_type=MESH)
 
     for i in (0, 1, 2, 3, 6):
         loads[i].wait()
@@ -296,11 +303,21 @@
         back[d] = pltpu.make_async_remote_copy(
             bsend.at[slot_of(behind[d])], brecv.at[z], bs.at[d], br.at[d], device_id=zback[d], device_id_type=MESH
         )
-    for d in OFFSETS:
-        @pl.when(ahead_earlier[d])
-        def _(d=d):
-            for copy in out[d]:
-                copy.start()
+    def send_to(j):
+        d = (j - z) & (NZ - 1)
+        for src, dst, ss, rs in ((csend, crecv, cs, cr), (send, recv, ps, pr)):
+            pltpu.make_async_remote_copy(
+                src.at[j], dst.at[slot], ss.at[d], rs.at[d], device_id=at(y, j, c), device_id_type=MESH
+            ).start()
+
+    for j in range(HALF):
+        pl.when(precedes[j])(functools.partial(send_to, j))
+
+    @pl.when(lone)
+    def _():
+        for j in near_lone:
+            send_to(j)
+
 
     eye = iota((64, 128), 0) == iota((64, 128), 1)
     hsend[0] = jnp.sum(jnp.where(eye, field[:, 255:256], 0.0), axis=0, keepdims=True)
@@ -312,6 +329,8 @@
         hsend.at[1], hrecv.at[1], hs.at[1], hr.at[1], device_id=before, device_id_type=MESH
     )
 
+    pl.semaphore_wait(wready.at[2], 1)
+    weights[2].start()
     pl.when(i_last)(to_after.start)
     pl.when(b_first)(to_before.start)
 
@@ -334,30 +353,30 @@
         ]
 
     def send_on(d):
-        goes = jnp.logical_and(jnp.logical_and(early, ahead_later[d]), jnp.logical_not(ahead_last[d]))
-
-        @pl.when(jnp.logical_and(goes, jnp.logical_not(relayed)) if d in FAR else goes)
+        @pl.when(jnp.logical_and(z + d < NZ, jnp.logical_not(relayed)) if d in FAR else z + d < NZ)
         def _():
             pl.semaphore_wait(ready.at[d], 1)
             for copy in out[d]:
                 copy.start()
 
-    for d in (*range(1, GROUP + 2), *range(NZ - 1, FAR[-1], -1), *range(FAR[-1], GROUP + 1, -1)):
-        send_on(d)
-        if d == GROUP:
-            @pl.when(relayed)
-            def _():
-                for copy in bundle:
-                    copy.start()
-
-        if d in onward:
-            @pl.when(relays)
-            def _(d=d):
-                if d == 1:
+    @pl.when(early)
+    def _():
+        for d in (*range(1, GROUP + 2), *range(NZ - 1, FAR[-1], -1), *range(FAR[-1], GROUP + 1, -1)):
+            send_on(d)
+            if d == GROUP:
+                @pl.when(relayed)
+                def _():
                     for copy in bundle:
-                        copy.wait_recv()
-                for copy in onward[d]:
-                    copy.start()
+                        copy.start()
+
+            if d in onward:
+                @pl.when(relays)
+                def _(d=d):
+                    if d == 1:
+                        for copy in bundle:
+                            copy.wait_recv()
+                    for copy in onward[d]:
+                        copy.start()
 
     @pl.when(relayed)
     def _():
@@ -384,15 +403,12 @@
     tell(z == HALF - 1, HALF + 1, range(1, GROUP + 1))
     tell(z == 1, NZ - 1, range(NZ - 2, NZ - 2 - GROUP, -1))
 
-    def send_alike():
+    @pl.when(lone)
+    def _():
         pl.semaphore_wait(allhere, 1)
-        for d in OFFSETS:
-            @pl.when(ahead_alike[d])
-            def _(d=d):
-                for copy in out[d]:
-                    copy.start()
-
-    pl.when(lone)(send_alike)
+        for j in range(HALF, HALF + GROUP):
+            send_to(j)
+
 
     @pl.when(later[4])
     def _():
@@ -432,10 +448,12 @@
     for k in (1, 3, 2):
         weights[k].wait_recv()
         weights[k + 4].start()
-    for k in (1, 3, 2, 4, 5, 7, 6):
-        if k >= 4:
-            weights[k].wait_recv()
-        gbuf[k] = product(wbuf[k, 0:128, :], wbuf[k, 128:192, :])
+    for ks in ((1, 3, 2), (4, 5, 7, 6)):
+        for k in ks:
+            if k >= 4:
+                weights[k].wait_recv()
+        for k in ks:
+            gbuf[k] = product(wbuf[k, 0:128, :], wbuf[k, 128:192, :])
 
     spreads = table[...]
     for start, stop in ((0, GROUP), (GROUP, HALF + 1), (HALF + 1, NZ + 1)):
@@ -444,7 +462,7 @@
         for j in sources:
             @pl.when(jnp.logical_and(z != j, apply[j]))
             def _(j=j):
-                d = lax.rem(z - j + NZ, NZ)
+                d = (z - j) & (NZ - 1)
                 for src, dst, ss, rs in ((csend, crecv, cs, cr), (send, recv, ps, pr)):
                     pltpu.make_async_remote_copy(
                         src.at[j], dst.at[j], ss.at[d], rs.at[d], device_id=at(y, j, c), device_id_type=MESH
@@ -458,13 +476,21 @@
         for j in sources:
             @pl.when(jnp.logical_and(z != j, apply[j]))
             def _(j=j):
-                d = lax.rem(z - j + NZ, NZ)
+                d = (z - j) & (NZ - 1)
                 pltpu.make_async_remote_copy(
                     bsend.at[slot_of(j)], brecv.at[z], bs.at[d], br.at[d], device_id=at(y, j, c), device_id_type=MESH
                 ).start()
 
         if start == 0:
-            pl.when(late)(send_alike)
+            @pl.when(late)
+            def _():
+                pl.semaphore_wait(allhere, 1)
+                for j in range(HALF, NZ):
+                    pl.when(z != j)(functools.partial(send_to, j))
+
+                @pl.when(jnp.logical_and(special, middle))
+                def _():
+                    send_to(0)
 
             @pl.when(jnp.logical_or(tells_after, tells_before))
             def _():
@@ -472,12 +498,13 @@
                 for d in range(1, NZ - 1):
                     pl.semaphore_signal(rowhere, inc=1, device_id=zpeer[d], device_id_type=MESH)
 
-            for d in OFFSETS:
-                @pl.when(jnp.logical_and(ahead_last[d], jnp.logical_and(z != 1, z != HALF - 1)))
-                def _(d=d):
-                    pl.semaphore_wait(ready.at[d], 1)
-                    for copy in out[d]:
-                        copy.start()
+            others = jnp.logical_and(jnp.logical_and(z > 1, z != HALF - 1), jnp.logical_not(middle))
+
+            @pl.when(jnp.logical_and(special, others))
+            def _():
+                pl.semaphore_wait(ready.at[(NZ - z) & (NZ - 1)], 1)
+                send_to(0)
+
     brecv[z] = bsend[slot]
 
     @pl.when(jnp.logical_and(b_last, z == 0))

time: 32 us -> 31 us (0.969)
  Pallas kernels: 31.2 us -> 30.1 us
    pallas_call x1, Pallas kernels: 31.2 us -> 30.1 us  [body(): pl.pallas_call(kernel, out_shape=jax.ShapeDtypeStruct((64, 256), F32), in...]
where the time goes in v7:
time: 31 us; the launch traced here: 30.7 us
  Pallas kernels  30.1 us (97%)
  local copies, waits for them, and re-layouts  0.63 us (2%)
    pallas_call x1, Pallas kernels, body(): pl.pallas_call(kernel, out_shape=jax.ShapeDtypeStruct((64, 256), F32), in...  30.1 us
    unnamed x1, local copies, waits for them, and re-layouts  0.63 us

profile of v7, /device:TPU:24, one launch (start us, length us, event | category | flops | bytes accessed | tf_op | source)
XLA Modules:
  0.0 30.7 jit_solution(10339658372432520056)
XLA Ops:
  0.0 30.1 %regroup_solve.1 = f32[64,256]{1,0:T(8,128)S(1)} custom-call(f32[64,256]{1,0:T(8,128)} %pot_hbm.1, s32[1,256]{1,0:T(1,128)} %bitcast.7, s32[1,256]{1,0:T(1,128)} %bitcast.8, s32[1,256]{1,0:T(1,128)} %bitcast.9, bf16[256,64]{1,0:T(8,128)(2,1)} %bitcast.5, bf16[64,64]{1,0:T(8,128)(2,1)} %bitcast.6, f32[8]{0:T(128)} %skin_hbm.1), custom_call_target="tpu_custom_call" | custom-call | tf_op jit(solution)/shard_map/regroup_solve/pallas_call | solution.py:569
  30.1 0.6 %copy.9 = f32[64,256]{1,0:T(8,128)} copy(f32[64,256]{1,0:T(8,128)S(1)} %regroup_solve.1) | data formatting | bytes 131072

commit v8 on v7

--- a/solution.py
+++ b/solution.py
@@ -167,7 +167,11 @@
     b_first = jnp.logical_and(has_before, jnp.logical_and(behind_next, jnp.logical_not(part_before)))
     b_last = jnp.logical_and(has_before, jnp.logical_not(behind_next))
     relayed = mine < GROUP
-    relays = jnp.logical_and(jnp.logical_and(z >= GROUP, z < 2 * GROUP), turn_of(z - GROUP) < GROUP)
+    relays = jnp.logical_and(z >= GROUP, z <= GROUP + 2)
+    present = [
+        jnp.logical_or(z == GROUP + 1, z == GROUP + 2),
+        jnp.logical_or(z == GROUP + 1, jnp.logical_and(z == GROUP, jnp.logical_not(special))),
+    ]
 
     barrier = pltpu.get_barrier_semaphore()
     @pl.when(early)
@@ -334,49 +338,71 @@
     pl.when(i_last)(to_after.start)
     pl.when(b_first)(to_before.start)
 
-    span = pl.ds(lax.rem(z + FAR[0], NZ - len(FAR) + 1), len(FAR))
+    span = pl.ds(jnp.minimum(z + FAR[0], NZ - len(FAR)), len(FAR))
+    via, half_of = GROUP + ((z + 1) >> 1), (z + 1) & 1
     bundle = [
         pltpu.make_async_remote_copy(
-            src.at[span], dst, bds.at[i], bdr.at[i], device_id=zpeer[GROUP], device_id_type=MESH
+            src.at[span], dst.at[half_of], bds.at[i], bdr.at[2 * half_of + i],
+            device_id=at(y, via, c), device_id_type=MESH,
         )
         for i, (src, dst) in enumerate([(csend, crbuf), (send, rbuf)])
     ]
-    from_slot = slot_of(jnp.maximum(z - GROUP, 0))
-    onward = {}
-    for j in range(1, len(FAR) + 1):
-        onward[j] = [
+
+    def onward(b, i):
+        source = jnp.clip(2 * (z - GROUP) - 1 + b, 0, GROUP - 1)
+        to = source + FAR[0] + i
+        return [
             pltpu.make_async_remote_copy(
-                src.at[j - 1], dst.at[from_slot], ss.at[j - 1], rs.at[j + GROUP],
-                device_id=zpeer[j], device_id_type=MESH,
+                src.at[b, i], dst.at[source], ss.at[b * len(FAR) + i], rs.at[to - source],
+                device_id=at(y, to, c), device_id_type=MESH,
             )
             for src, dst, ss, rs in ((crbuf, crecv, cfs, cr), (rbuf, recv, fs, pr))
         ]
+
+    def send_onward(d):
+        for b in range(2):
+            i = d - b - (z - GROUP)
+
+            @pl.when(jnp.logical_and(present[b], jnp.logical_and(i >= 0, i < len(FAR))))
+            def _(b=b, i=i):
+                for copy in onward(b, jnp.clip(i, 0, len(FAR) - 1)):
+                    copy.start()
 
     def send_on(d):
         @pl.when(jnp.logical_and(z + d < NZ, jnp.logical_not(relayed)) if d in FAR else z + d < NZ)
         def _():
             pl.semaphore_wait(ready.at[d], 1)
-            for copy in out[d]:
-                copy.start()
-
-    @pl.when(early)
-    def _():
-        for d in (*range(1, GROUP + 2), *range(NZ - 1, FAR[-1], -1), *range(FAR[-1], GROUP + 1, -1)):
-            send_on(d)
-            if d == GROUP:
-                @pl.when(relayed)
+            if d in (3, 4):
+                @pl.when(jnp.logical_and(relayed, via - z == d))
                 def _():
                     for copy in bundle:
                         copy.start()
 
-            if d in onward:
-                @pl.when(relays)
-                def _(d=d):
-                    if d == 1:
-                        for copy in bundle:
-                            copy.wait_recv()
-                    for copy in onward[d]:
-                        copy.start()
+            if GROUP <= d <= GROUP + 3:
+                pl.when(relays)(functools.partial(send_onward, d))
+            for copy in out[d]:
+                copy.start()
+
+    @pl.when(early)
+    def _():
+        for d in range(1, GROUP):
+            send_on(d)
+        for b in range(2):
+            @pl.when(present[b])
+            def _(b=b):
+                for i, buffer in enumerate((crbuf, rbuf)):
+                    pltpu.make_async_remote_copy(
+                        buffer.at[b], buffer.at[b], bds.at[i], bdr.at[2 * b + i],
+                        device_id=zpeer[1], device_id_type=MESH,
+                    ).wait_recv()
+
+        @pl.when(relays)
+        def _():
+            for d in range(GROUP - 1, 0, -1):
+                send_onward(d)
+
+        for d in (*range(GROUP, HALF), *range(NZ - 1, HALF - 1, -1)):
+            send_on(d)
 
     @pl.when(relayed)
     def _():
@@ -459,7 +485,7 @@
     for start, stop in ((0, GROUP), (GROUP, HALF + 1), (HALF + 1, NZ + 1)):
         sources = [j for j in range(NZ) if start <= j + (j >= HALF) < stop] + ([0] if start == GROUP else [])
         apply = {j: (special if start == GROUP else jnp.logical_not(special)) if j == 0 else True for j in sources}
-        for j in sources:
+        for j in reversed(sources):
             @pl.when(jnp.logical_and(z != j, apply[j]))
             def _(j=j):
                 d = (z - j) & (NZ - 1)
@@ -549,11 +575,12 @@
         for copy in bundle:
             copy.wait_send()
 
-    @pl.when(relays)
-    def _():
-        for j in onward:
-            for copy in onward[j]:
-                copy.wait_send()
+    for b in range(2):
+        @pl.when(present[b])
+        def _(b=b):
+            for i in range(len(FAR)):
+                for copy in onward(b, i):
+                    copy.wait_send()
 
     pl.when(has_after)(to_after.wait_send)
     pl.when(has_before)(to_before.wait_send)
@@ -591,8 +618,8 @@
             pltpu.VMEM((NZ + 1, 1, 128), F32),
             pltpu.VMEM((2, 1, 128), F32),
             pltpu.VMEM((2, 1, 128), F32),
-            pltpu.VMEM((len(FAR), 16, 128), BF16),
-            pltpu.VMEM((len(FAR), 1, 128), F32),
+            pltpu.VMEM((2, len(FAR), 16, 128), BF16),
+            pltpu.VMEM((2, len(FAR), 1, 128), F32),
             dma((7,)),
             pltpu.SemaphoreType.REGULAR((NZ,)),
             pltpu.SemaphoreType.REGULAR((8,)),
@@ -601,8 +628,9 @@
             pltpu.SemaphoreType.REGULAR,
             *[dma((NZ,)) for _ in range(6)],
             *[dma((8,)) for _ in range(2)],
-            *[dma((2,)) for _ in range(4)],
-            *[dma((len(FAR),)) for _ in range(2)],
+            *[dma((2,)) for _ in range(3)],
+            dma((4,)),
+            *[dma((2 * len(FAR),)) for _ in range(2)],
         ],
         compiler_params=pltpu.CompilerParams(
             collective_id=0, has_side_effects=True, vmem_limit_bytes=32 * 1024 * 1024

time: 31 us -> 30.9 us (level)
  no operation moved by 1% of the time
where the time goes in v8:
time: 30.9 us; the launch traced here: 30.6 us
  Pallas kernels  30 us (97%)
  local copies, waits for them, and re-layouts  0.63 us (2%)
    pallas_call x1, Pallas kernels, body(): pl.pallas_call(kernel, out_shape=jax.ShapeDtypeStruct((64, 256), F32), in...  30 us
    unnamed x1, local copies, waits for them, and re-layouts  0.63 us

profile of v8, /device:TPU:24, one launch (start us, length us, event | category | flops | bytes accessed | tf_op | source)
XLA Modules:
  0.0 30.6 jit_solution(4459708938919671679)
XLA Ops:
  0.0 30.0 %regroup_solve.1 = f32[64,256]{1,0:T(8,128)S(1)} custom-call(f32[64,256]{1,0:T(8,128)} %pot_hbm.1, s32[1,256]{1,0:T(1,128)} %bitcast.7, s32[1,256]{1,0:T(1,128)} %bitcast.8, s32[1,256]{1,0:T(1,128)} %bitcast.9, bf16[256,64]{1,0:T(8,128)(2,1)} %bitcast.5, bf16[64,64]{1,0:T(8,128)(2,1)} %bitcast.6, f32[8]{0:T(128)} %skin_hbm.1), custom_call_target="tpu_custom_call" | custom-call | tf_op jit(solution)/shard_map/regroup_solve/pallas_call | solution.py:596
  30.0 0.6 %copy.9 = f32[64,256]{1,0:T(8,128)} copy(f32[64,256]{1,0:T(8,128)S(1)} %regroup_solve.1) | data formatting | bytes 131072

commit v9 on v7

--- a/solution.py
+++ b/solution.py
@@ -62,7 +62,13 @@
     return mm(levels, jnp.concatenate([c, c], axis=0)).astype(BF16)
 
 
-def solve(points, codes, wbuf, gbuf, table, total):
+def natural(a, b):
+    low = iota((128, 128), 1) < 64
+    a, b = a.astype(F32), b.astype(F32)
+    return jnp.concatenate([jnp.where(low, a, turn(b)), jnp.where(low, turn(a), b)], axis=0).astype(BF16)
+
+
+def solve(points, codes, abuf, gbuf, table, total):
     n = codes.shape[0]
     rows = 16 * n
     row, lane = iota((rows, 128), 0), iota((rows, 128), 1)
@@ -94,8 +100,11 @@
         sides.append((c < 0.0, (jnp.abs(c) > 128.0) != first))
         upper = sides[h][0]
         d2 = jnp.where(first, x, xr) if h == 0 else jnp.where(first, xr, x)
-        blocks = jnp.concatenate([wbuf[h * 4 + p, 0:128, :] for p in range(4)], axis=1)
-        ys.append(doubled(mm(by_pair(jnp.where(upper != first, d2, 0.0)), blocks, NT), sides[h][1]))
+        own = jnp.concatenate(
+            [jnp.where(pair == 2 * q + lane // 64, d2, 0.0).astype(BF16) for q in range(2)], axis=1
+        )
+        got = mm(own, jnp.concatenate([abuf[2 * h], abuf[2 * h + 1]], axis=1), NT)
+        ys.append(doubled(jnp.where(upper, got[:, 128:256], got[:, 0:128]), sides[h][1]))
 
     def coupled(v, h):
         return mm(v, jnp.concatenate([gbuf[h * 4 + p] for p in range(4)], axis=1), NT)
@@ -118,7 +127,7 @@
 
 def kernel(
     pot_hbm, types_hbm, sat_hbm, pat_hbm, inv_hbm, cpl_hbm, skin_hbm, out_ref,
-    pot, typ, sat, pat, inv, cpl, skin, place, table, wbuf, gbuf, send, recv, bsend, brecv, csend, crecv, hsend, hrecv, rbuf, crbuf,
+    pot, typ, sat, pat, inv, cpl, skin, place, table, wbuf, gbuf, abuf, send, recv, bsend, brecv, csend, crecv, hsend, hrecv, rbuf, crbuf,
     load_sem, ready, wready, hready, allhere, rowhere, ps, pr, cs, cr, bs, br, ws, wr, hs, hr, bds, bdr, fs, cfs,
 ):
     dom, x = lax.axis_index("dom"), lax.axis_index("cell")
@@ -454,12 +463,15 @@
                 weights[k].wait_recv()
         for k in ks:
             gbuf[k] = product(wbuf[k, 0:128, :], wbuf[k, 128:192, :])
+        for q in range(2):
+            k = 0 if 1 in ks else 4
+            abuf[k // 2 + q] = natural(wbuf[k + 2 * q, 0:128, :], wbuf[k + 2 * q + 1, 0:128, :])
 
     spreads = table[...]
     for start, stop in ((0, GROUP), (GROUP, HALF + 1), (HALF + 1, NZ + 1)):
         sources = [j for j in range(NZ) if start <= j + (j >= HALF) < stop] + ([0] if start == GROUP else [])
         apply = {j: (special if start == GROUP else jnp.logical_not(special)) if j == 0 else True for j in sources}
-        for j in sources:
+        for j in reversed(sources):
             @pl.when(jnp.logical_and(z != j, apply[j]))
             def _(j=j):
                 d = (z - j) & (NZ - 1)
@@ -470,7 +482,7 @@
 
         n = stop - start
         answer = solve(
-            recv[start:stop].reshape(n * 16, 128), crecv[start:stop].reshape(n, 128), wbuf, gbuf, spreads, total
+            recv[start:stop].reshape(n * 16, 128), crecv[start:stop].reshape(n, 128), abuf, gbuf, spreads, total
         )
         bsend[start:stop] = answer.reshape(n, 16, 128)
         for j in sources:
@@ -583,6 +595,7 @@
             pltpu.VMEM((128, 768), BF16),
             pltpu.VMEM((8, 192, 128), BF16),
             pltpu.VMEM((8, 256, 128), BF16),
+            pltpu.VMEM((4, 256, 128), BF16),
             pltpu.VMEM((NZ, 16, 128), BF16),
             pltpu.VMEM((NZ + 1, 16, 128), BF16),
             pltpu.VMEM((NZ + 1, 16, 128), BF16),

time: 31 us -> 31 us (level)
  no operation moved by 1% of the time
where the time goes in v9:
time: 31 us; the launch traced here: 30.7 us
  Pallas kernels  30.1 us (97%)
  local copies, waits for them, and re-layouts  0.63 us (2%)
    pallas_call x1, Pallas kernels, body(): pl.pallas_call(kernel, out_shape=jax.ShapeDtypeStruct((64, 256), F32), in...  30.1 us
    unnamed x1, local copies, waits for them, and re-layouts  0.63 us

profile of v9, /device:TPU:24, one launch (start us, length us, event | category | flops | bytes accessed | tf_op | source)
XLA Modules:
  0.0 30.7 jit_solution(16714167117549839232)
XLA Ops:
  0.0 30.1 %regroup_solve.1 = f32[64,256]{1,0:T(8,128)S(1)} custom-call(f32[64,256]{1,0:T(8,128)} %pot_hbm.1, s32[1,256]{1,0:T(1,128)} %bitcast.7, s32[1,256]{1,0:T(1,128)} %bitcast.8, s32[1,256]{1,0:T(1,128)} %bitcast.9, bf16[256,64]{1,0:T(8,128)(2,1)} %bitcast.5, bf16[64,64]{1,0:T(8,128)(2,1)} %bitcast.6, f32[8]{0:T(128)} %skin_hbm.1), custom_call_target="tpu_custom_call" | custom-call | tf_op jit(solution)/shard_map/regroup_solve/pallas_call | solution.py:581
  30.1 0.6 %copy.9 = f32[64,256]{1,0:T(8,128)} copy(f32[64,256]{1,0:T(8,128)S(1)} %regroup_solve.1) | data formatting | bytes 131072
